TPU v7x, 128 devices: a whole 4x4x4 slice. The times are simulated.
128 devices in a mesh: group: 8 (over z, core), tp: 16 (over x, y).
Axes of the slice: x: 4, y: 4, z: 4, core: 2. Of those that a mesh axis runs over, the one named last changes fastest.
Arguments:
- hidden_inputs: bfloat16 [3072, 2, 8192], P('group', None, 'tp'), may hold values from -6 to 6
- base_matrix: bfloat16 [8192, 8192], P(None, 'tp'), may hold values from -0.0625 to 0.0625
- adapter_down: bfloat16 [64, 64, 8192], P('group', None, 'tp'), may hold values from -0.0625 to 0.0625
- adapter_up: bfloat16 [64, 64, 8192], P('group', None, 'tp'), may hold values from -0.75 to 0.75
- adapter_ranks: int32 [64], replicated, may hold values from 16 to 64
- adapter_pages: int32 [64], replicated, may hold values from 0 to 63, as said below
- row_adapters: int32 [3072], P('group'), may hold values from 0 to 63, as said below
Outputs:
- adapted_rows: bfloat16 [3072, 2, 8192], P('group', None, 'tp')
Inputs may be any that keep to these rules, and one draw needn't show every extreme that they name: `adapter_pages`: a permutation: every adapter has its own page slot; slot s lies with group s // 8. `row_adapters`: in each group's aligned block of 384 rows, at most 96 rows name adapters whose page slots lie with any one group, and exactly 96 rows do so for some group in every block.
All inputs are finite; a program needn't handle non-finite values.
Results may differ from a plain program's by a relative error of at most 0.0044.
Values may be sent and summed in bfloat16 or wider, within the bound.
No kernel may reach another device: no remote copies, remote signals or barrier semaphores. Data moves between devices by JAX's collectives and lax.ppermute only.
A program may use at most 128 MiB of HBM per device.

v0:
```python
import jax
import jax.numpy as jnp
from jax import lax
from jax.sharding import PartitionSpec as P


def lookup(table, index):
    onehot = index[:, None] == jnp.arange(table.shape[0], dtype=jnp.int32)[None, :]
    return jnp.sum(jnp.where(onehot, table[None, :], 0), axis=1)


def adapter_apply(features, page_slot_index, rank_value, down_pages, up_pages):
    row_combined, step_counter, shard_width = features.shape
    page_count, rank_width = (down_pages.shape[0], down_pages.shape[1])
    flat_rows = features.reshape(row_combined * step_counter, shard_width)
    down_flat = down_pages.reshape(page_count * rank_width, shard_width)
    scores = lax.dot_general(
        flat_rows, down_flat, (((1,), (1,)), ((), ())), preferred_element_type=jnp.float32
    )
    scores = scores.reshape(row_combined, step_counter, page_count, rank_width)
    picked = page_slot_index[:, None] == jnp.arange(page_count, dtype=jnp.int32)[None, :]
    partial_sum = jnp.sum(jnp.where(picked[:, None, :, None], scores, 0.0), axis=2)
    rank_sum = lax.psum(partial_sum, "tp")
    rank_mask = jnp.arange(rank_width, dtype=jnp.int32)[None, :] < rank_value[:, None]
    row_scale = 32.0 / rank_value.astype(jnp.float32)
    reduced = jnp.where(rank_mask[:, None, :], rank_sum * row_scale[:, None, None], 0.0).astype(
        jnp.bfloat16
    )
    broadcast_rows = jnp.where(
        picked[:, None, :, None], reduced[:, :, None, :], jnp.zeros((), jnp.bfloat16)
    )
    broadcast_rows = broadcast_rows.reshape(row_combined * step_counter, page_count * rank_width)
    up_flattened = up_pages.reshape(page_count * rank_width, shard_width)
    adapter_output = jnp.dot(broadcast_rows, up_flattened, preferred_element_type=jnp.float32)
    return adapter_output.reshape(row_combined, step_counter, shard_width).astype(jnp.bfloat16)


def per_device(
    hidden_inputs, base_matrix, adapter_down, adapter_up, adapter_ranks, adapter_pages, row_adapters
):
    row_count, step_counter, feature_width = hidden_inputs.shape
    initial = jnp.zeros((row_count, step_counter, base_matrix.shape[1]), jnp.float32)
    piece = lax.all_gather(hidden_inputs, "tp", axis=2, tiled=True)
    flat_rows = piece.reshape(-1, piece.shape[2])
    base_output = jnp.dot(flat_rows, base_matrix, preferred_element_type=jnp.float32).reshape(
        initial.shape
    )
    slot_for_row = lookup(adapter_pages, row_adapters)
    rank_vector = lookup(adapter_ranks, row_adapters)
    down_every, up_every = (
        lax.all_gather(adapter_down, "group", axis=0, tiled=True),
        lax.all_gather(adapter_up, "group", axis=0, tiled=True),
    )
    adapter_output = adapter_apply(hidden_inputs, slot_for_row, rank_vector, down_every, up_every)
    return (base_output + adapter_output.astype(jnp.float32)).astype(jnp.bfloat16)


def solution(mesh):
    return jax.shard_map(
        per_device,
        mesh=mesh,
        in_specs=(
            P("group", None, "tp"),
            P(None, "tp"),
            P("group", None, "tp"),
            P("group", None, "tp"),
            P(),
            P(),
            P("group"),
        ),
        out_specs=P("group", None, "tp"),
        check_vma=False,
    )
```

profile of v0, /device:TPU:102, one launch (start us, length us, event | category | flops | bytes accessed | tf_op | source)
XLA Modules:
  0.0 287.3 jit_solution(13547653840780305411)
XLA Ops:
  6.5 0.0 all-gather.6.cloned.1.call-start
  6.5 0.7 all-gather.6.cloned.1.call-update
  7.3 0.0 all-reduce.2.cloned.1.call-start
  7.3 0.8 select_reduce_fusion.1
  8.1 32.4 %all-gather.6.cloned.1.call-done = bf16[64,64,512]{2,1,0:T(8,128)(2,1)} async-done(((bf16[8,64,512]{2,1,0:T(8,128)(2,1)}), bf16[64,64,512]{2,1,0:T(8,128)(2,1)}) %all-gather.6.cloned.1.call-update) | async-done | bytes 4194320 | tf_op jit(solution)/shard_map/all_gather | solution.py:51
  40.5 0.0 copy-start
  40.5 6.7 %select_reduce_fusion = f32[384,2,64]{0,2,1:T(8,128)} fusion(pred[384,64]{0,1:T(8,128)(4,1)S(1)} %iota_compare_fusion.1, bf16[64,64,512]{2,1,0:T(8,128)(2,1)} %all-gather.6.cloned.1.call-done, bf16[384,2,512,1]{2,1,0,3:T(2,128)(2,1)} %bitcast.20), kind=kOutput, calls=%fused_computation | convolution fusion | flops 3227467776 | bytes 5201920 | tf_op jit(solution)/shard_map/dot_general | solution.py:17
  47.1 0.0 all-reduce.2.cloned.1.call-update
  47.2 0.0 all-gather.8.cloned.1.call-start
  47.2 0.7 all-gather.8.cloned.1.call-update
  47.9 0.0 all-gather.4.cloned.1.call-start
  48.0 0.0 copy-done
  48.0 1.0 copy.12
  48.9 0.0 all-gather.4.cloned.1.call-update
  49.0 83.2 %all-reduce.2.cloned.1.call-done = f32[384,2,64]{0,2,1:T(8,128)} async-done(((f32[384,2,64]{0,2,1:T(8,128)}), f32[384,2,64]{0,2,1:T(8,128)}) %all-reduce.2.cloned.1.call-update) | async-done | bytes 196624 | tf_op jit(solution)/shard_map/psum | solution.py:23
  132.2 1.0 select_convert_fusion
  133.1 30.7 %all-gather.8.cloned.1.call-done = bf16[64,64,512]{2,1,0:T(8,128)(2,1)} async-done(((bf16[8,64,512]{2,1,0:T(8,128)(2,1)}), bf16[64,64,512]{2,1,0:T(8,128)(2,1)}) %all-gather.8.cloned.1.call-update) | async-done | bytes 4194320 | tf_op jit(solution)/shard_map/all_gather | solution.py:52
  163.9 5.6 %bitcast_convert_fusion = bf16[384,2,512]{2,0,1:T(8,128)(2,1)S(1)} fusion(bf16[64,64,512]{2,1,0:T(8,128)(2,1)} %all-gather.8.cloned.1.call-done, pred[384,64]{0,1:T(8,128)(4,1)S(1)} %iota_compare_fusion.1, bf16[384,2,64]{0,2,1:T(8,128)(2,1)S(1)} %select_convert_fusion), kind=kOutput, calls=%fused_computation.11 | convolution fusion | flops 3224764416 | bytes 5103616 | tf_op jit(solution)/shard_map/dot_general | solution.py:34
  169.5 97.6 %all-gather.4.cloned.1.call-done = bf16[384,2,8192]{2,0,1:T(8,128)(2,1)} async-done(((bf16[384,2,512]{2,0,1:T(8,128)(2,1)}), bf16[384,2,8192]{2,0,1:T(8,128)(2,1)}) %all-gather.4.cloned.1.call-update) | async-done | bytes 12582928 | tf_op jit(solution)/shard_map/all_gather | solution.py:43
  267.1 12.0 %add_convert_fusion = bf16[384,2,512]{2,0,1:T(8,128)(2,1)S(1)} fusion(bf16[384,2,512]{2,0,1:T(8,128)(2,1)S(1)} %bitcast_convert_fusion, bf16[384,2,8192]{2,0,1:T(8,128)(2,1)} %all-gather.4.cloned.1.call-done, bf16[8192,512]{1,0:T(8,128)(2,1)} %param.8), kind=kOutput, calls=%fused_computation.12 | convolution fusion | flops 6443630592 | bytes 22544384 | tf_op jit(solution)/shard_map/dot_general | solution.py:45
  279.1 1.7 copy.14
  (3 shorter events, 0.0 us)
Async XLA Ops:
  6.5 33.9 %all-gather.6.cloned.1.call-start = ((), (), s32[]{:S(2)}) async-start(), calls=%async_computation.1 | async-start | bytes 4718592 | tf_op jit(solution)/shard_map/all_gather | solution.py:51
  7.3 124.9 %all-reduce.2.cloned.1.call-start = ((), (), s32[]{:S(2)}) async-start(), calls=%async_computation.2 | async-start | bytes 393216 | tf_op jit(solution)/shard_map/psum | solution.py:23
  40.5 7.5 %copy-start = (bf16[384,2,512]{2,1,0:T(2,128)(2,1)S(1)}, bf16[384,2,512]{2,1,0:T(2,128)(2,1)}, u32[]{:S(2)}) copy-start(bf16[384,2,512]{2,1,0:T(2,128)(2,1)} %param.7) | copy-start | bytes 2359300
  47.2 116.7 %all-gather.8.cloned.1.call-start = ((), (), s32[]{:S(2)}) async-start(), calls=%async_computation.3 | async-start | bytes 4718592 | tf_op jit(solution)/shard_map/all_gather | solution.py:52
  47.9 219.2 %all-gather.4.cloned.1.call-start = ((), (), s32[]{:S(2)}) async-start(), calls=%async_computation | async-start | bytes 13369344 | tf_op jit(solution)/shard_map/all_gather | solution.py:43
Sparse Core Ops, SparseCore 0:
  9.1 31.3 all-gather.5
  47.3 84.8 all-reduce.1
  133.9 29.9 all-gather.7
  165.8 101.1 all-gather.3
where the time goes:
time: 289 us; the launch traced here: 287 us
  waiting for transfers between devices  245 us (85%)
  matrix products  24.3 us (8%)
  between operations  13.2 us (5%)
    all_gather x1, waiting for transfers between devices, per_device(): piece = lax.all_gather(hidden_inputs, 'tp', axis=2, tiled=True)  97.6 us
    psum x1, waiting for transfers between devices, adapter_apply(): rank_sum = lax.psum(partial_sum, 'tp')  83.2 us
    all_gather x1, waiting for transfers between devices, per_device(): lax.all_gather(adapter_down, 'group', axis=0, tiled=True)  32.4 us
    all_gather x1, waiting for transfers between devices, per_device(): lax.all_gather(adapter_up, 'group', axis=0, tiled=True)  30.7 us
    dot_general x1, matrix products, per_device(): jnp.dot(flat_rows, base_matrix, preferred_element_type=jnp.float32)  12 us
    dot_general x1, matrix products, adapter_apply(): lax.dot_general(flat_rows, down_flat, (((1,), (1,)), ((), ())), preferred...  6.66 us
  transfers between devices with their start and end apart: 4, of which 4 were waited for; matrix products, arithmetic and copies ran while one was open for 3% of the time, Pallas kernels for 0%

commit v1 on v0

v1 whole, which is shorter than its diff:
```python
import jax
import jax.numpy as jnp
from jax import lax
from jax.sharding import PartitionSpec as P

SIDE = 4
BOTH = ("group", "tp")


def sign_of(core):
    return 1 if core == 0 else -1


def shift_pairs(dx, dy):
    pairs = []
    for group in range(8):
        sign = sign_of(group % 2)
        for x in range(SIDE):
            for y in range(SIDE):
                to = ((x + sign * dx) % SIDE) * SIDE + (y + sign * dy) % SIDE
                pairs.append((group * 16 + x * SIDE + y, group * 16 + to))
    return pairs


def shift(value, dx, dy):
    return lax.ppermute(value, BOTH, shift_pairs(dx, dy))


def gather_chunks(own):
    got = {(0, 0): own}
    got[1, 0] = shift(own, 1, 0)
    got[0, 1] = shift(own, 0, 1)
    got[-1, 0] = shift(own, -1, 0)
    got[0, -1] = shift(own, 0, -1)
    got[2, 0] = shift(got[1, 0], 1, 0)
    got[0, 2] = shift(got[0, 1], 0, 1)
    got[1, 1] = shift(got[0, 1], 1, 0)
    got[-1, 1] = shift(got[-1, 0], 0, 1)
    got[-1, -1] = shift(got[0, -1], -1, 0)
    got[1, -1] = shift(got[1, 0], 0, -1)
    got[1, 2] = shift(got[0, 2], 1, 0)
    got[-1, 2] = shift(got[0, 2], -1, 0)
    got[2, 1] = shift(got[2, 0], 0, 1)
    got[2, -1] = shift(got[2, 0], 0, -1)
    half = own.shape[0] // 2
    first = shift(got[1, 2][:half], 1, 0)
    second = shift(got[2, 1][half:], 0, 1)
    got[2, 2] = jnp.concatenate([first, second], axis=0)
    return got


def lookup(table, index):
    onehot = index[:, None] == jnp.arange(table.shape[0], dtype=jnp.int32)[None, :]
    return jnp.sum(jnp.where(onehot, table[None, :], 0), axis=1)


def per_device(
    hidden_inputs, base_matrix, adapter_down, adapter_up, adapter_ranks, adapter_pages, row_adapters
):
    row_count, steps, width = hidden_inputs.shape
    flat_count = row_count * steps
    tp_index = lax.axis_index("tp")
    sign = 1 - 2 * (lax.axis_index("group") % 2)
    place_x, place_y = tp_index // SIDE, tp_index % SIDE
    tp_size = SIDE * SIDE

    rows = hidden_inputs.reshape(flat_count, width)
    chunks = gather_chunks(rows)

    down_every = lax.all_gather(adapter_down, "group", axis=0, tiled=True)
    up_every = lax.all_gather(adapter_up, "group", axis=0, tiled=True)
    pages, rank_width = down_every.shape[:2]

    slot = jnp.repeat(lookup(adapter_pages, row_adapters), steps)
    rank = jnp.repeat(lookup(adapter_ranks, row_adapters), steps)
    picked = slot[:, None] == jnp.arange(pages, dtype=jnp.int32)[None, :]
    scores = lax.dot_general(
        rows,
        down_every.reshape(pages * rank_width, width),
        (((1,), (1,)), ((), ())),
        preferred_element_type=jnp.float32,
    ).reshape(flat_count, pages, rank_width)
    partial = jnp.sum(jnp.where(picked[:, :, None], scores, 0.0), axis=1)
    share = flat_count // tp_size
    parts = lax.all_to_all(
        partial.reshape(tp_size, share, rank_width), "tp", 0, 0, tiled=True
    )
    rank_sum = jnp.sum(parts, axis=0)
    own_rank = lax.dynamic_slice(rank, (tp_index * share,), (share,))
    mask = jnp.arange(rank_width, dtype=jnp.int32)[None, :] < own_rank[:, None]
    scale = 32.0 / own_rank.astype(jnp.float32)
    own_reduced = jnp.where(mask, rank_sum * scale[:, None], 0.0).astype(jnp.bfloat16)
    reduced = lax.all_to_all(
        jnp.broadcast_to(own_reduced[None], (tp_size, share, rank_width)), "tp", 0, 0, tiled=True
    ).reshape(flat_count, rank_width)
    spread = jnp.where(picked[:, :, None], reduced[:, None, :], jnp.zeros((), jnp.bfloat16))
    lora = jnp.dot(
        spread.reshape(flat_count, pages * rank_width),
        up_every.reshape(pages * rank_width, width),
        preferred_element_type=jnp.float32,
    ).astype(jnp.bfloat16)

    base = None
    for (dx, dy), chunk in chunks.items():
        source = ((place_x - sign * dx) % SIDE) * SIDE + (place_y - sign * dy) % SIDE
        block = lax.dynamic_slice(base_matrix, (source * width, 0), (width, base_matrix.shape[1]))
        term = jnp.dot(chunk, block, preferred_element_type=jnp.float32)
        base = term if base is None else base + term
    return (base + lora.astype(jnp.float32)).astype(jnp.bfloat16).reshape(hidden_inputs.shape)


def solution(mesh):
    return jax.shard_map(
        per_device,
        mesh=mesh,
        in_specs=(
            P("group", None, "tp"),
            P(None, "tp"),
            P("group", None, "tp"),
            P("group", None, "tp"),
            P(),
            P(),
            P("group"),
        ),
        out_specs=P("group", None, "tp"),
        check_vma=False,
    )
```

time: 289 us -> 154 us (0.53)
  waiting for transfers between devices: 245 us -> 36.2 us
  starting transfers between devices: 0.12 us -> 33.7 us
  matrix products: 24.3 us -> 51.4 us
  local copies, waits for them, and re-layouts: 2.65 us -> 13.1 us
    all_gather x3 -> x2, waiting for transfers between devices: 161 us -> 0.02 us  [the longest x1 0.02 us: per_device(): up_every = lax.all_gather(adapter_up, 'group', axis=0, tiled=True)]
    psum x1 -> x0, waiting for transfers between devices: 83.2 us -> none  [adapter_apply(): rank_sum = lax.psum(partial_sum, 'tp')]
    ppermute x0 -> x16, waiting for transfers between devices: none -> 29.1 us  [shift(): return lax.ppermute(value, BOTH, shift_pairs(dx, dy))]
    dot_general x3 -> x18, matrix products: 24.3 us -> 51.4 us  [the longest x16 39 us: per_device(): term = jnp.dot(chunk, block, preferred_element_type=jnp.float32)]
    ppermute x0 -> x16, starting transfers between devices: none -> 20.7 us  [shift(): return lax.ppermute(value, BOTH, shift_pairs(dx, dy))]
    all_to_all x0 -> x2, starting transfers between devices: none -> 12.9 us  [the longest x1 7.21 us: per_device(): lax.all_to_all(partial.reshape(tp_size, share, rank_width), 'tp', 0, 0, t...]
    all_to_all x0 -> x2, waiting for transfers between devices: none -> 5.62 us  [the longest x1 3.01 us: per_device(): lax.all_to_all(partial.reshape(tp_size, share, rank_width), 'tp', 0, 0, t...]
    unnamed x3 -> x44, local copies, waits for them, and re-layouts: 0.96 us -> 5.14 us
  transfers between devices with their start and end apart: 4 -> 20, of which waited for: 4 -> 8; matrix products, arithmetic and copies ran while one was open for 3% -> 39% of each run, Pallas kernels for 0% -> 0%
where the time goes in v1:
time: 154 us; the launch traced here: 152 us
  matrix products  51.4 us (33%)
  waiting for transfers between devices  36.2 us (24%)
  starting transfers between devices  33.7 us (22%)
  between operations  13.9 us (9%)
  local copies, waits for them, and re-layouts  13.1 us (9%)
  other arithmetic  3.45 us (2%)
    dot_general x16, matrix products, per_device(): term = jnp.dot(chunk, block, preferred_element_type=jnp.float32)  39 us
    ppermute x16, waiting for transfers between devices, shift(): return lax.ppermute(value, BOTH, shift_pairs(dx, dy))  29.1 us
    ppermute x16, starting transfers between devices, shift(): return lax.ppermute(value, BOTH, shift_pairs(dx, dy))  20.7 us
    all_to_all x1, starting transfers between devices, per_device(): lax.all_to_all(partial.reshape(tp_size, share, rank_width), 'tp', 0, 0, t...  7.21 us
    dot_general x1, matrix products, per_device(): lax.dot_general(rows, down_every.reshape(pages * rank_width, width), (((1...  6.6 us
    dot_general x1, matrix products, per_device(): jnp.dot(spread.reshape(flat_count, pages * rank_width), up_every.reshape(...  5.8 us
    all_to_all x1, starting transfers between devices, per_device(): lax.all_to_all(jnp.broadcast_to(own_reduced[None], (tp_size, share, rank_...  5.7 us
    unnamed x44, local copies, waits for them, and re-layouts  5.14 us
  transfers between devices with their start and end apart: 20, of which 8 were waited for; matrix products, arithmetic and copies ran while one was open for 39% of the time, Pallas kernels for 0%

profile of v1, /device:TPU:102, one launch (start us, length us, event | category | flops | bytes accessed | tf_op | source)
XLA Modules:
  0.0 151.6 jit_solution(8975185565416706234)
XLA Ops:
  8.4 1.6 %collective-permute-start.1 = (bf16[768,512]{1,0:T(8,128)(2,1)S(1)}, bf16[768,512]{1,0:T(8,128)(2,1)}, u32[]{:S(2)}, u32[]{:S(2)}) collective-permute-start(bf16[768,512]{1,0:T(8,128)(2,1)S(1)} %reshape.80), channel_id=1, source_target_pairs={{0,1},{1,2},{2,3},{3,0},{4,5},{5,6},{6,7},{7,4},{8,9},{9,10},{10,1... | collective-permute-start | bytes 2359304 | tf_op jit(solution)/shard_map/ppermute | solution.py:26
  10.0 1.7 %collective-permute-start.3 = (bf16[768,512]{1,0:T(8,128)(2,1)S(1)}, bf16[768,512]{1,0:T(8,128)(2,1)}, u32[]{:S(2)}, u32[]{:S(2)}) collective-permute-start(bf16[768,512]{1,0:T(8,128)(2,1)S(1)} %reshape.80), channel_id=1, source_target_pairs={{0,3},{1,0},{2,1},{3,2},{4,7},{5,4},{6,5},{7,6},{8,11},{9,8},{10,9... | collective-permute-start | bytes 2359304 | tf_op jit(solution)/shard_map/ppermute | solution.py:26
  11.7 0.8 collective-permute-start.2
  12.5 2.4 %collective-permute-start = (bf16[768,512]{1,0:T(8,128)(2,1)S(1)}, bf16[768,512]{1,0:T(8,128)(2,1)}, u32[]{:S(2)}, u32[]{:S(2)}) collective-permute-start(bf16[768,512]{1,0:T(8,128)(2,1)S(1)} %reshape.80), channel_id=1, source_target_pairs={{0,4},{1,5},{2,6},{3,7},{4,8},{5,9},{6,10},{7,11},{8,12},{9,13},{1... | collective-permute-start | bytes 2359304 | tf_op jit(solution)/shard_map/ppermute | solution.py:26
  14.9 1.2 reshape.84
  17.0 1.8 %fusion.44 = f32[512,768]{1,0:T(8,128)S(1)} fusion(bf16[768,512]{1,0:T(8,128)(2,1)S(1)} %reshape.80, bf16[8192,512]{1,0:T(8,128)(2,1)} %param.8, s32[]{:T(128)S(6)} %select_n.173), kind=kOutput, calls=%fused_computation.43 | convolution fusion | flops 402653184 | bytes 2883588 | tf_op jit(solution)/shard_map/dot_general | solution.py:107
  18.8 9.7 %collective-permute-done.1 = bf16[768,512]{1,0:T(8,128)(2,1)} collective-permute-done((bf16[768,512]{1,0:T(8,128)(2,1)S(1)}, bf16[768,512]{1,0:T(8,128)(2,1)}, u32[]{:S(2)}, u32[]{:S(2)}) %collective-permute-start.1) | collective-permute-done | bytes 786464 | tf_op jit(solution)/shard_map/ppermute | solution.py:26
  29.0 1.7 %collective-permute-start.5 = (bf16[768,512]{1,0:T(8,128)(2,1)}, bf16[768,512]{1,0:T(8,128)(2,1)}, u32[]{:S(2)}, u32[]{:S(2)}) collective-permute-start(bf16[768,512]{1,0:T(8,128)(2,1)} %collective-permute-done.1), channel_id=1, source_target_pairs={{0,1},{1,2},{2,3},{3,0},{4,5},{5,6},{6,7},{7,4},{8,9},{9,10},{10,1... | collective-permute-start | bytes 2359304 | tf_op jit(solution)/shard_map/ppermute | solution.py:26
  30.7 1.5 %collective-permute-start.8 = (bf16[768,512]{1,0:T(8,128)(2,1)}, bf16[768,512]{1,0:T(8,128)(2,1)S(1)}, u32[]{:S(2)}, u32[]{:S(2)}) collective-permute-start(bf16[768,512]{1,0:T(8,128)(2,1)} %collective-permute-done.3), channel_id=1, source_target_pairs={{0,12},{1,13},{2,14},{3,15},{4,0},{5,1},{6,2},{7,3},{8,4},{9,5},{1... | collective-permute-start | bytes 2359304 | tf_op jit(solution)/shard_map/ppermute | solution.py:26
  32.8 0.8 collective-permute-start.7
  33.6 1.2 collective-permute-start.4
  34.9 1.9 %fusion.42 = f32[512,768]{1,0:T(8,128)S(1)} fusion(bf16[768,512]{1,0:T(8,128)(2,1)} %collective-permute-done, bf16[8192,512]{1,0:T(8,128)(2,1)} %param.8, s32[]{:T(128)S(6)} %select_n.176), kind=kOutput, calls=%fused_computation.41 | convolution fusion | flops 402653184 | bytes 2883588 | tf_op jit(solution)/shard_map/dot_general | solution.py:107
  36.8 3.1 %fusion.40 = f32[512,768]{1,0:T(8,128)} fusion(bf16[768,512]{1,0:T(8,128)(2,1)} %collective-permute-done.1, bf16[8192,512]{1,0:T(8,128)(2,1)} %param.8, s32[]{:T(128)S(6)} %select_n.178), kind=kOutput, calls=%fused_computation.39 | convolution fusion | flops 402653184 | bytes 2883588 | tf_op jit(solution)/shard_map/dot_general | solution.py:107
  39.9 3.0 %fusion.38 = f32[512,768]{1,0:T(8,128)} fusion(bf16[768,512]{1,0:T(8,128)(2,1)} %collective-permute-done.2, bf16[8192,512]{1,0:T(8,128)(2,1)S(1)} %copy-done, s32[]{:T(128)S(6)} %select_n.180), kind=kOutput, calls=%fused_computation.37 | convolution fusion | flops 402653184 | bytes 2883588 | tf_op jit(solution)/shard_map/dot_general | solution.py:107
  42.8 2.9 %fusion.36 = f32[512,768]{1,0:T(8,128)} fusion(bf16[768,512]{1,0:T(8,128)(2,1)} %collective-permute-done.3, bf16[8192,512]{1,0:T(8,128)(2,1)S(1)} %copy-done, s32[]{:T(128)S(6)} %select_n.182), kind=kOutput, calls=%fused_computation.35 | convolution fusion | flops 402653184 | bytes 2883588 | tf_op jit(solution)/shard_map/dot_general | solution.py:107
  45.7 2.4 %collective-permute-start.9 = (bf16[768,512]{1,0:T(8,128)(2,1)}, bf16[768,512]{1,0:T(8,128)(2,1)S(1)}, u32[]{:S(2)}, u32[]{:S(2)}) collective-permute-start(bf16[768,512]{1,0:T(8,128)(2,1)} %collective-permute-done), channel_id=1, source_target_pairs={{0,3},{1,0},{2,1},{3,2},{4,7},{5,4},{6,5},{7,6},{8,11},{9,8},{10,9... | collective-permute-start | bytes 2359304 | tf_op jit(solution)/shard_map/ppermute | solution.py:26
  48.1 2.9 %fusion.32 = f32[512,768]{1,0:T(8,128)} fusion(bf16[768,512]{1,0:T(8,128)(2,1)} %collective-permute-done.5, bf16[8192,512]{1,0:T(8,128)(2,1)S(1)} %copy-done, s32[]{:T(128)S(6)} %select_n.186), kind=kOutput, calls=%fused_computation.31 | convolution fusion | flops 402653184 | bytes 2883588 | tf_op jit(solution)/shard_map/dot_general | solution.py:107
  51.0 1.6 %collective-permute-done.8 = bf16[768,512]{1,0:T(8,128)(2,1)S(1)} collective-permute-done((bf16[768,512]{1,0:T(8,128)(2,1)}, bf16[768,512]{1,0:T(8,128)(2,1)S(1)}, u32[]{:S(2)}, u32[]{:S(2)}) %collective-permute-start.8) | collective-permute-done | bytes 786464 | tf_op jit(solution)/shard_map/ppermute | solution.py:26
  52.9 1.8 %fusion.26 = f32[512,768]{1,0:T(8,128)} fusion(bf16[768,512]{1,0:T(8,128)(2,1)S(1)} %collective-permute-done.8, bf16[8192,512]{1,0:T(8,128)(2,1)S(1)} %copy-done, s32[]{:T(128)S(6)} %select_n.189), kind=kOutput, calls=%fused_computation.25 | convolution fusion | flops 402653184 | bytes 2883588 | tf_op jit(solution)/shard_map/dot_general | solution.py:107
  54.7 6.6 %collective-permute-done.4 = bf16[768,512]{1,0:T(8,128)(2,1)} collective-permute-done((bf16[768,512]{1,0:T(8,128)(2,1)}, bf16[768,512]{1,0:T(8,128)(2,1)}, u32[]{:S(2)}, u32[]{:S(2)}) %collective-permute-start.4) | collective-permute-done | bytes 786464 | tf_op jit(solution)/shard_map/ppermute | solution.py:26
  61.4 2.9 %fusion.34 = f32[512,768]{1,0:T(8,128)} fusion(bf16[768,512]{1,0:T(8,128)(2,1)} %collective-permute-done.4, bf16[8192,512]{1,0:T(8,128)(2,1)S(1)} %copy-done, s32[]{:T(128)S(6)} %select_n.184), kind=kOutput, calls=%fused_computation.33 | convolution fusion | flops 402653184 | bytes 2883588 | tf_op jit(solution)/shard_map/dot_general | solution.py:107
  64.3 4.0 %collective-permute-start.12 = (bf16[768,512]{1,0:T(8,128)(2,1)}, bf16[768,512]{1,0:T(8,128)(2,1)S(1)}, u32[]{:S(2)}, u32[]{:S(2)}) collective-permute-start(bf16[768,512]{1,0:T(8,128)(2,1)} %collective-permute-done.4), channel_id=1, source_target_pairs={{0,1},{1,2},{2,3},{3,0},{4,5},{5,6},{6,7},{7,4},{8,9},{9,10},{10,1... | collective-permute-start | bytes 2359304 | tf_op jit(solution)/shard_map/ppermute | solution.py:26
  68.2 1.8 %fusion.28 = f32[512,768]{1,0:T(8,128)} fusion(bf16[768,512]{1,0:T(8,128)(2,1)S(1)} %collective-permute-done.7, bf16[8192,512]{1,0:T(8,128)(2,1)S(1)} %copy-done, s32[]{:T(128)S(6)} %select_n.188), kind=kOutput, calls=%fused_computation.27 | convolution fusion | flops 402653184 | bytes 2883588 | tf_op jit(solution)/shard_map/dot_general | solution.py:107
  70.0 1.8 %fusion.30 = f32[512,768]{1,0:T(8,128)} fusion(bf16[768,512]{1,0:T(8,128)(2,1)S(1)} %collective-permute-done.6, bf16[8192,512]{1,0:T(8,128)(2,1)S(1)} %copy-done, s32[]{:T(128)S(6)} %select_n.187), kind=kOutput, calls=%fused_computation.29 | convolution fusion | flops 402653184 | bytes 2883588 | tf_op jit(solution)/shard_map/dot_general | solution.py:107
  71.8 1.8 %fusion.24 = f32[512,768]{1,0:T(8,128)} fusion(bf16[768,512]{1,0:T(8,128)(2,1)S(1)} %collective-permute-done.9, bf16[8192,512]{1,0:T(8,128)(2,1)S(1)} %copy-done, s32[]{:T(128)S(6)} %select_n.190), kind=kOutput, calls=%fused_computation.23 | convolution fusion | flops 402653184 | bytes 2883588 | tf_op jit(solution)/shard_map/dot_general | solution.py:107
  73.6 0.8 collective-permute-done.10
  74.4 0.8 slice.8
  75.2 1.7 %collective-permute-start.14 = (bf16[384,512]{1,0:T(8,128)(2,1)}, bf16[384,512]{1,0:T(8,128)(2,1)}, u32[]{:S(2)}, u32[]{:S(2)}) collective-permute-start(bf16[384,512]{1,0:T(8,128)(2,1)} %slice.8), channel_id=1, source_target_pairs={{0,4},{1,5},{2,6},{3,7},{4,8},{5,9},{6,10},{7,11},{8,12},{9,13},{1... | collective-permute-start | bytes 1179656 | tf_op jit(solution)/shard_map/ppermute | solution.py:26
  76.9 9.8 %collective-permute-done.12 = bf16[768,512]{1,0:T(8,128)(2,1)S(1)} collective-permute-done((bf16[768,512]{1,0:T(8,128)(2,1)}, bf16[768,512]{1,0:T(8,128)(2,1)S(1)}, u32[]{:S(2)}, u32[]{:S(2)}) %collective-permute-start.12) | collective-permute-done | bytes 786464 | tf_op jit(solution)/shard_map/ppermute | solution.py:26
  87.5 1.8 %fusion.22 = f32[512,768]{1,0:T(8,128)} fusion(bf16[768,512]{1,0:T(8,128)(2,1)S(1)} %collective-permute-done.10, bf16[8192,512]{1,0:T(8,128)(2,1)S(1)} %copy-done, s32[]{:T(128)S(6)} %select_n.191), kind=kOutput, calls=%fused_computation.21 | convolution fusion | flops 402653184 | bytes 2883588 | tf_op jit(solution)/shard_map/dot_general | solution.py:107
  89.3 1.8 %fusion.18 = f32[512,768]{1,0:T(8,128)} fusion(bf16[768,512]{1,0:T(8,128)(2,1)S(1)} %collective-permute-done.12, bf16[8192,512]{1,0:T(8,128)(2,1)S(1)} %copy-done, s32[]{:T(128)S(6)} %select_n.193), kind=kOutput, calls=%fused_computation.17 | convolution fusion | flops 402653184 | bytes 2883588 | tf_op jit(solution)/shard_map/dot_general | solution.py:107
  91.1 6.6 %select_reduce_fusion = f32[768,64]{0,1:T(8,128)} fusion(pred[768,64]{0,1:T(8,128)(4,1)S(1)} %iota_compare_fusion, bf16[768,512,1]{1,0,2:T(8,128)(2,1)} %reshape.84, bf16[64,64,512]{2,1,0:T(8,128)(2,1)} %all-gather.3.cloned.1.call-done), kind=kOutput, calls=%fused_computation | convolution fusion | flops 3227467776 | bytes 5226496 | tf_op jit(solution)/shard_map/dot_general | solution.py:77
  97.7 1.1 copy.45
  98.8 0.9 reshape.87
  99.7 7.2 %all-to-all-start = ((f32[16,1,3072]{2,1,0:T(1,128)}), f32[16,1,3072]{2,1,0:T(1,128)S(1)}, u32[]{:S(2)}, u32[]{:S(2)}) async-start(f32[16,1,3072]{2,1,0:T(1,128)} %reshape.87), calls=%async_computation | async-start | bytes 393216 | tf_op jit(solution)/shard_map/all_to_all | solution.py:85
  106.9 3.1 %fusion.20 = f32[512,768]{1,0:T(8,128)} fusion(bf16[768,512]{1,0:T(8,128)(2,1)} %collective-permute-done.11, bf16[8192,512]{1,0:T(8,128)(2,1)} %param.8, s32[]{:T(128)S(6)} %select_n.192), kind=kOutput, calls=%fused_computation.19 | convolution fusion | flops 402653184 | bytes 2883588 | tf_op jit(solution)/shard_map/dot_general | solution.py:107
  110.0 3.0 %all-to-all-done = f32[16,1,3072]{2,1,0:T(1,128)S(1)} async-done(((f32[16,1,3072]{2,1,0:T(1,128)}), f32[16,1,3072]{2,1,0:T(1,128)S(1)}, u32[]{:S(2)}, u32[]{:S(2)}) %all-to-all-start) | async-done | bytes 196640 | tf_op jit(solution)/shard_map/all_to_all | solution.py:85
  113.6 1.8 %reduce = f32[16,3072]{1,0:T(8,128)} reduce(f32[16,1,3072]{2,1,0:T(1,128)S(1)} %all-to-all-done, f32[]{:T(128)} %broadcast.48), dimensions={1}, to_apply=%all_to_all.6.reduce_sub_computation | reduce | bytes 393220 | tf_op jit(solution)/shard_map/all_to_all | solution.py:85
  115.3 1.0 reshape.88
  117.0 0.8 select_convert_fusion
  117.9 0.8 reshape.89
  118.7 5.7 %all-to-all-start.1 = ((bf16[16,2,1536]{2,1,0:T(2,128)(2,1)}), bf16[16,2,1536]{2,1,0:T(2,128)(2,1)S(1)}, u32[]{:S(2)}, u32[]{:S(2)}) async-start(bf16[16,2,1536]{2,1,0:T(2,128)(2,1)} %reshape.89), calls=%async_computation.1 | async-start | bytes 196608 | tf_op jit(solution)/shard_map/all_to_all | solution.py:93
  124.4 3.1 %fusion.9 = f32[768,512]{0,1:T(8,128)} fusion(bf16[384,512]{1,0:T(8,128)(2,1)} %collective-permute-done.15, bf16[384,512]{1,0:T(8,128)(2,1)} %collective-permute-done.14, bf16[8192,512]{1,0:T(8,128)(2,1)} %param.8, s32[]{:T(128)S(6)} %select_n.195), kind=kOutput, calls=%fused_computation.10 | convolution fusion | flops 404226048 | bytes 2883588 | tf_op jit(solution)/shard_map/dot_general | solution.py:107
  127.5 2.6 %all-to-all-done.1 = bf16[16,2,1536]{2,1,0:T(2,128)(2,1)S(1)} async-done(((bf16[16,2,1536]{2,1,0:T(2,128)(2,1)}), bf16[16,2,1536]{2,1,0:T(2,128)(2,1)S(1)}, u32[]{:S(2)}, u32[]{:S(2)}) %all-to-all-start.1) | async-done | bytes 98336 | tf_op jit(solution)/shard_map/all_to_all | solution.py:93
  130.6 5.8 %bitcast_convert_fusion = bf16[768,512]{0,1:T(8,128)(2,1)S(1)} fusion(bf16[64,64,512]{2,1,0:T(8,128)(2,1)} %all-gather.5.cloned.1.call-done, pred[768,64]{0,1:T(8,128)(4,1)S(1)} %copy-done.16, bf16[768,64]{0,1:T(8,128)(2,1)S(1)} %copy.46), kind=kOutput, calls=%fused_computation.6 | convolution fusion | flops 3224764416 | bytes 5128192 | tf_op jit(solution)/shard_map/dot_general | solution.py:97
  138.6 3.6 %fusion.6 = bf16[768,512]{0,1:T(8,128)(2,1)} fusion(f32[768,512]{0,1:T(8,128)S(1)} %copy-done.13, f32[512,768]{1,0:T(8,128)S(1)} %copy-done.11, f32[512,768]{1,0:T(8,128)S(1)} %copy-done.12, f32[512,768]{1,0:T(8,128)S(1)} %copy-done.10, f32[512,768]{1,0:T(8,128)S(1)} %copy-done.9, f32[512,768]{1,0:T(8,128)S(1)} %copy-done.5, f32[512,768]{1,0:T(8,128)S(1)} %copy-done.7, ...), kind=kOutput, calls=%fused_computation.9 | convolution fusion | flops 409731072 | bytes 26476548 | tf_op jit(solution)/shard_map/dot_general | solution.py:107
  142.2 1.4 copy.42
  143.6 1.2 reshape.83
  (76 shorter events, 8.4 us)
Async XLA Ops:
  6.5 1.5 copy-start.14
  6.5 84.5 %all-gather.3.cloned.1.call-start = ((), (), s32[]{:S(2)}) async-start(), calls=%async_computation.2 | async-start | bytes 4718592 | tf_op jit(solution)/shard_map/all_gather | solution.py:70
  7.3 123.2 %all-gather.5.cloned.1.call-start = ((), (), s32[]{:S(2)}) async-start(), calls=%async_computation.3 | async-start | bytes 4718592 | tf_op jit(solution)/shard_map/all_gather | solution.py:71
  8.0 8.1 %copy-start.17 = (s32[384]{0:T(512)S(1)}, s32[384]{0:T(512)}, u32[]{:S(2)}) copy-start(s32[384]{0:T(512)} %param.13) | copy-start | bytes 4612
  8.0 8.0 %copy-start.18 = (s32[64]{0:T(128)S(1)}, s32[64]{0:T(128)}, u32[]{:S(2)}) copy-start(s32[64]{0:T(128)} %param.11) | copy-start | bytes 772
  8.0 8.0 %copy-start.19 = (s32[64]{0:T(128)S(1)}, s32[64]{0:T(128)}, u32[]{:S(2)}) copy-start(s32[64]{0:T(128)} %param.12) | copy-start | bytes 772
  8.4 20.1 %collective-permute-start.1 = (bf16[768,512]{1,0:T(8,128)(2,1)S(1)}, bf16[768,512]{1,0:T(8,128)(2,1)}, u32[]{:S(2)}, u32[]{:S(2)}) collective-permute-start(bf16[768,512]{1,0:T(8,128)(2,1)S(1)} %reshape.80), channel_id=1, source_target_pairs={{0,1},{1,2},{2,3},{3,0},{4,5},{5,6},{6,7},{7,4},{8,9},{9,10},{10,1... | collective-permute-start | bytes 2359304 | tf_op jit(solution)/shard_map/ppermute | solution.py:26
  10.0 20.7 %collective-permute-start.3 = (bf16[768,512]{1,0:T(8,128)(2,1)S(1)}, bf16[768,512]{1,0:T(8,128)(2,1)}, u32[]{:S(2)}, u32[]{:S(2)}) collective-permute-start(bf16[768,512]{1,0:T(8,128)(2,1)S(1)} %reshape.80), channel_id=1, source_target_pairs={{0,3},{1,0},{2,1},{3,2},{4,7},{5,4},{6,5},{7,6},{8,11},{9,8},{10,9... | collective-permute-start | bytes 2359304 | tf_op jit(solution)/shard_map/ppermute | solution.py:26
  11.7 21.1 %collective-permute-start.2 = (bf16[768,512]{1,0:T(8,128)(2,1)S(1)}, bf16[768,512]{1,0:T(8,128)(2,1)}, u32[]{:S(2)}, u32[]{:S(2)}) collective-permute-start(bf16[768,512]{1,0:T(8,128)(2,1)S(1)} %reshape.80), channel_id=1, source_target_pairs={{0,12},{1,13},{2,14},{3,15},{4,0},{5,1},{6,2},{7,3},{8,4},{9,5},{1... | collective-permute-start | bytes 2359304 | tf_op jit(solution)/shard_map/ppermute | solution.py:26
  12.5 21.1 %collective-permute-start = (bf16[768,512]{1,0:T(8,128)(2,1)S(1)}, bf16[768,512]{1,0:T(8,128)(2,1)}, u32[]{:S(2)}, u32[]{:S(2)}) collective-permute-start(bf16[768,512]{1,0:T(8,128)(2,1)S(1)} %reshape.80), channel_id=1, source_target_pairs={{0,4},{1,5},{2,6},{3,7},{4,8},{5,9},{6,10},{7,11},{8,12},{9,13},{1... | collective-permute-start | bytes 2359304 | tf_op jit(solution)/shard_map/ppermute | solution.py:26
  16.9 74.2 %copy-start.15 = (pred[768,64]{0,1:T(8,128)(4,1)}, pred[768,64]{0,1:T(8,128)(4,1)S(1)}, u32[]{:S(2)}) copy-start(pred[768,64]{0,1:T(8,128)(4,1)S(1)} %iota_compare_fusion) | copy-start | bytes 147460
  16.9 22.9 %copy-start = (bf16[8192,512]{1,0:T(8,128)(2,1)S(1)}, bf16[8192,512]{1,0:T(8,128)(2,1)}, u32[]{:S(2)}) copy-start(bf16[8192,512]{1,0:T(8,128)(2,1)} %param.8) | copy-start | bytes 25165828
  28.5 41.5 %collective-permute-start.6 = (bf16[768,512]{1,0:T(8,128)(2,1)}, bf16[768,512]{1,0:T(8,128)(2,1)S(1)}, u32[]{:S(2)}, u32[]{:S(2)}) collective-permute-start(bf16[768,512]{1,0:T(8,128)(2,1)} %collective-permute-done.1), channel_id=1, source_target_pairs={{0,4},{1,5},{2,6},{3,7},{4,8},{5,9},{6,10},{7,11},{8,12},{9,13},{1... | collective-permute-start | bytes 2359304 | tf_op jit(solution)/shard_map/ppermute | solution.py:26
  29.0 16.8 %collective-permute-start.5 = (bf16[768,512]{1,0:T(8,128)(2,1)}, bf16[768,512]{1,0:T(8,128)(2,1)}, u32[]{:S(2)}, u32[]{:S(2)}) collective-permute-start(bf16[768,512]{1,0:T(8,128)(2,1)} %collective-permute-done.1), channel_id=1, source_target_pairs={{0,1},{1,2},{2,3},{3,0},{4,5},{5,6},{6,7},{7,4},{8,9},{9,10},{10,1... | collective-permute-start | bytes 2359304 | tf_op jit(solution)/shard_map/ppermute | solution.py:26
  30.7 21.9 %collective-permute-start.8 = (bf16[768,512]{1,0:T(8,128)(2,1)}, bf16[768,512]{1,0:T(8,128)(2,1)S(1)}, u32[]{:S(2)}, u32[]{:S(2)}) collective-permute-start(bf16[768,512]{1,0:T(8,128)(2,1)} %collective-permute-done.3), channel_id=1, source_target_pairs={{0,12},{1,13},{2,14},{3,15},{4,0},{5,1},{6,2},{7,3},{8,4},{9,5},{1... | collective-permute-start | bytes 2359304 | tf_op jit(solution)/shard_map/ppermute | solution.py:26
  32.8 31.5 %collective-permute-start.7 = (bf16[768,512]{1,0:T(8,128)(2,1)}, bf16[768,512]{1,0:T(8,128)(2,1)S(1)}, u32[]{:S(2)}, u32[]{:S(2)}) collective-permute-start(bf16[768,512]{1,0:T(8,128)(2,1)} %collective-permute-done.2), channel_id=1, source_target_pairs={{0,1},{1,2},{2,3},{3,0},{4,5},{5,6},{6,7},{7,4},{8,9},{9,10},{10,1... | collective-permute-start | bytes 2359304 | tf_op jit(solution)/shard_map/ppermute | solution.py:26
  33.6 27.7 %collective-permute-start.4 = (bf16[768,512]{1,0:T(8,128)(2,1)}, bf16[768,512]{1,0:T(8,128)(2,1)}, u32[]{:S(2)}, u32[]{:S(2)}) collective-permute-start(bf16[768,512]{1,0:T(8,128)(2,1)} %collective-permute-done), channel_id=1, source_target_pairs={{0,4},{1,5},{2,6},{3,7},{4,8},{5,9},{6,10},{7,11},{8,12},{9,13},{1... | collective-permute-start | bytes 2359304 | tf_op jit(solution)/shard_map/ppermute | solution.py:26
  45.7 26.1 %collective-permute-start.9 = (bf16[768,512]{1,0:T(8,128)(2,1)}, bf16[768,512]{1,0:T(8,128)(2,1)S(1)}, u32[]{:S(2)}, u32[]{:S(2)}) collective-permute-start(bf16[768,512]{1,0:T(8,128)(2,1)} %collective-permute-done), channel_id=1, source_target_pairs={{0,3},{1,0},{2,1},{3,2},{4,7},{5,4},{6,5},{7,6},{8,11},{9,8},{10,9... | collective-permute-start | bytes 2359304 | tf_op jit(solution)/shard_map/ppermute | solution.py:26
  52.6 54.3 %collective-permute-start.11 = (bf16[768,512]{1,0:T(8,128)(2,1)}, bf16[768,512]{1,0:T(8,128)(2,1)}, u32[]{:S(2)}, u32[]{:S(2)}) collective-permute-start(bf16[768,512]{1,0:T(8,128)(2,1)} %collective-permute-done.5), channel_id=1, source_target_pairs={{0,12},{1,13},{2,14},{3,15},{4,0},{5,1},{6,2},{7,3},{8,4},{9,5},{1... | collective-permute-start | bytes 2359304 | tf_op jit(solution)/shard_map/ppermute | solution.py:26
  61.4 13.0 %collective-permute-start.10 = (bf16[768,512]{1,0:T(8,128)(2,1)}, bf16[768,512]{1,0:T(8,128)(2,1)S(1)}, u32[]{:S(2)}, u32[]{:S(2)}) collective-permute-start(bf16[768,512]{1,0:T(8,128)(2,1)} %collective-permute-done.5), channel_id=1, source_target_pairs={{0,4},{1,5},{2,6},{3,7},{4,8},{5,9},{6,10},{7,11},{8,12},{9,13},{1... | collective-permute-start | bytes 2359304 | tf_op jit(solution)/shard_map/ppermute | solution.py:26
  64.3 22.4 %collective-permute-start.12 = (bf16[768,512]{1,0:T(8,128)(2,1)}, bf16[768,512]{1,0:T(8,128)(2,1)S(1)}, u32[]{:S(2)}, u32[]{:S(2)}) collective-permute-start(bf16[768,512]{1,0:T(8,128)(2,1)} %collective-permute-done.4), channel_id=1, source_target_pairs={{0,1},{1,2},{2,3},{3,0},{4,5},{5,6},{6,7},{7,4},{8,9},{9,10},{10,1... | collective-permute-start | bytes 2359304 | tf_op jit(solution)/shard_map/ppermute | solution.py:26
  70.0 66.4 %collective-permute-start.13 = (bf16[768,512]{1,0:T(8,128)(2,1)}, bf16[768,512]{1,0:T(8,128)(2,1)}, u32[]{:S(2)}, u32[]{:S(2)}) collective-permute-start(bf16[768,512]{1,0:T(8,128)(2,1)} %collective-permute-done.4), channel_id=1, source_target_pairs={{0,3},{1,0},{2,1},{3,2},{4,7},{5,4},{6,5},{7,6},{8,11},{9,8},{10,9... | collective-permute-start | bytes 2359304 | tf_op jit(solution)/shard_map/ppermute | solution.py:26
  75.2 49.2 %collective-permute-start.14 = (bf16[384,512]{1,0:T(8,128)(2,1)}, bf16[384,512]{1,0:T(8,128)(2,1)}, u32[]{:S(2)}, u32[]{:S(2)}) collective-permute-start(bf16[384,512]{1,0:T(8,128)(2,1)} %slice.8), channel_id=1, source_target_pairs={{0,4},{1,5},{2,6},{3,7},{4,8},{5,9},{6,10},{7,11},{8,12},{9,13},{1... | collective-permute-start | bytes 1179656 | tf_op jit(solution)/shard_map/ppermute | solution.py:26
  87.5 37.0 %collective-permute-start.15 = (bf16[384,512]{1,0:T(8,128)(2,1)}, bf16[384,512]{1,0:T(8,128)(2,1)}, u32[]{:S(2)}, u32[]{:S(2)}) collective-permute-start(bf16[384,512]{1,0:T(8,128)(2,1)} %slice.9), channel_id=1, source_target_pairs={{0,1},{1,2},{2,3},{3,0},{4,5},{5,6},{6,7},{7,4},{8,9},{9,10},{10,1... | collective-permute-start | bytes 1179656 | tf_op jit(solution)/shard_map/ppermute | solution.py:26
  99.7 13.3 %all-to-all-start = ((f32[16,1,3072]{2,1,0:T(1,128)}), f32[16,1,3072]{2,1,0:T(1,128)S(1)}, u32[]{:S(2)}, u32[]{:S(2)}) async-start(f32[16,1,3072]{2,1,0:T(1,128)} %reshape.87), calls=%async_computation | async-start | bytes 393216 | tf_op jit(solution)/shard_map/all_to_all | solution.py:85
  118.7 11.4 %all-to-all-start.1 = ((bf16[16,2,1536]{2,1,0:T(2,128)(2,1)}), bf16[16,2,1536]{2,1,0:T(2,128)(2,1)S(1)}, u32[]{:S(2)}, u32[]{:S(2)}) async-start(bf16[16,2,1536]{2,1,0:T(2,128)(2,1)} %reshape.89), calls=%async_computation.1 | async-start | bytes 196608 | tf_op jit(solution)/shard_map/all_to_all | solution.py:93
  124.4 6.0 %copy-start.16 = (pred[768,64]{0,1:T(8,128)(4,1)S(1)}, pred[768,64]{0,1:T(8,128)(4,1)}, u32[]{:S(2)}) copy-start(pred[768,64]{0,1:T(8,128)(4,1)} %copy-done.15) | copy-start | bytes 147460
  130.5 5.9 %copy-start.1 = (f32[512,768]{1,0:T(8,128)S(1)}, f32[512,768]{1,0:T(8,128)}, u32[]{:S(2)}) copy-start(f32[512,768]{1,0:T(8,128)} %fusion.40) | copy-start | bytes 4718596
  130.5 5.9 %copy-start.2 = (f32[512,768]{1,0:T(8,128)S(1)}, f32[512,768]{1,0:T(8,128)}, u32[]{:S(2)}) copy-start(f32[512,768]{1,0:T(8,128)} %fusion.38) | copy-start | bytes 4718596
  130.5 5.9 %copy-start.3 = (f32[512,768]{1,0:T(8,128)S(1)}, f32[512,768]{1,0:T(8,128)}, u32[]{:S(2)}) copy-start(f32[512,768]{1,0:T(8,128)} %fusion.36) | copy-start | bytes 4718596
  130.5 5.9 %copy-start.4 = (f32[512,768]{1,0:T(8,128)S(1)}, f32[512,768]{1,0:T(8,128)}, u32[]{:S(2)}) copy-start(f32[512,768]{1,0:T(8,128)} %fusion.32) | copy-start | bytes 4718596
  130.5 5.9 %copy-start.5 = (f32[512,768]{1,0:T(8,128)S(1)}, f32[512,768]{1,0:T(8,128)}, u32[]{:S(2)}) copy-start(f32[512,768]{1,0:T(8,128)} %fusion.26) | copy-start | bytes 4718596
  130.5 5.9 %copy-start.6 = (f32[512,768]{1,0:T(8,128)S(1)}, f32[512,768]{1,0:T(8,128)}, u32[]{:S(2)}) copy-start(f32[512,768]{1,0:T(8,128)} %fusion.34) | copy-start | bytes 4718596
  130.5 5.9 %copy-start.7 = (f32[512,768]{1,0:T(8,128)S(1)}, f32[512,768]{1,0:T(8,128)}, u32[]{:S(2)}) copy-start(f32[512,768]{1,0:T(8,128)} %fusion.28) | copy-start | bytes 4718596
  130.5 5.9 %copy-start.8 = (f32[512,768]{1,0:T(8,128)S(1)}, f32[512,768]{1,0:T(8,128)}, u32[]{:S(2)}) copy-start(f32[512,768]{1,0:T(8,128)} %fusion.30) | copy-start | bytes 4718596
  130.5 6.3 %copy-start.9 = (f32[512,768]{1,0:T(8,128)S(1)}, f32[512,768]{1,0:T(8,128)}, u32[]{:S(2)}) copy-start(f32[512,768]{1,0:T(8,128)} %fusion.24) | copy-start | bytes 4718596
  130.5 6.7 %copy-start.10 = (f32[512,768]{1,0:T(8,128)S(1)}, f32[512,768]{1,0:T(8,128)}, u32[]{:S(2)}) copy-start(f32[512,768]{1,0:T(8,128)} %fusion.22) | copy-start | bytes 4718596
  130.6 7.2 %copy-start.11 = (f32[512,768]{1,0:T(8,128)S(1)}, f32[512,768]{1,0:T(8,128)}, u32[]{:S(2)}) copy-start(f32[512,768]{1,0:T(8,128)} %fusion.18) | copy-start | bytes 4718596
  130.6 7.6 %copy-start.12 = (f32[512,768]{1,0:T(8,128)S(1)}, f32[512,768]{1,0:T(8,128)}, u32[]{:S(2)}) copy-start(f32[512,768]{1,0:T(8,128)} %fusion.20) | copy-start | bytes 4718596
  130.6 8.0 %copy-start.13 = (f32[768,512]{0,1:T(8,128)S(1)}, f32[768,512]{0,1:T(8,128)}, u32[]{:S(2)}) copy-start(f32[768,512]{0,1:T(8,128)} %fusion.9) | copy-start | bytes 4718596
Sparse Core Ops, SparseCore 0:
  9.1 31.3 all-gather.2
  42.2 32.1 all-gather.4

commit v2 on v0

v2 whole, which is shorter than its diff:
```python
import functools

import jax
import jax.numpy as jnp
from jax import lax
from jax.experimental import pallas as pl
from jax.experimental.pallas import tpu as pltpu
from jax.sharding import PartitionSpec as P

SIDE = 4
BOTH = ("group", "tp")
VMEM_BYTES = 28 * 2**20
DOWN_BLOCK = 16
UP_BLOCK = 32
AHEAD = 3
WINDOW = 4


def shift_pairs(dx, dy):
    pairs = []
    for group in range(8):
        step_x, step_y = (-dy, -dx) if group % 2 else (dx, dy)
        for x in range(SIDE):
            for y in range(SIDE):
                to = (x + step_x) % SIDE * SIDE + (y + step_y) % SIDE
                pairs.append((group * 16 + x * SIDE + y, group * 16 + to))
    return pairs


def shift(value, dx, dy):
    return lax.ppermute(value, BOTH, shift_pairs(dx, dy))


def after(value, *others):
    return lax.optimization_barrier((value,) + others)[0]


def in_vmem(value):
    return pltpu.with_memory_space_constraint(value, pltpu.VMEM)


class Messages:
    def __init__(self):
        self.sent = []

    def send(self, value, dx, dy, waits=()):
        earlier = self.sent[-WINDOW:][:1] if len(self.sent) >= WINDOW else []
        self.sent.append(shift(after(value, *earlier, *waits), dx, dy))
        return self.sent[-1]


def place_of(name):
    index = lax.axis_index("tp")
    core = lax.axis_index("group") & 1
    step_x = jnp.where(core == 1, -name[1], name[0])
    step_y = jnp.where(core == 1, -name[0], name[1])
    x = ((index >> 2) + SIDE - step_x) & (SIDE - 1)
    y = ((index & (SIDE - 1)) + SIDE - step_y) & (SIDE - 1)
    return x * SIDE + y


def local_call(body, name, operands, out_shape, flops=0, scratch=()):
    return pl.pallas_call(
        body,
        in_specs=[pl.BlockSpec(memory_space=pltpu.VMEM)] * len(operands),
        out_specs=jax.tree.map(lambda _: pl.BlockSpec(memory_space=pltpu.VMEM), out_shape),
        out_shape=out_shape,
        scratch_shapes=scratch,
        compiler_params=pltpu.CompilerParams(vmem_limit_bytes=VMEM_BYTES),
        cost_estimate=pl.CostEstimate(flops=flops, bytes_accessed=2**20, transcendentals=0),
        name=name,
    )(*[in_vmem(value) for value in operands])


def flatten_body(hidden_ref, rows_ref, first_ref, second_ref):
    rows = hidden_ref[...].reshape(rows_ref.shape)
    half = rows.shape[0] // 2
    rows_ref[...] = rows
    first_ref[...] = rows[:half]
    second_ref[...] = rows[half:]


def flatten(hidden):
    rows, steps, width = hidden.shape
    count = rows * steps
    shapes = [pltpu.VMEM((size, width), hidden.dtype) for size in (count, count // 2, count // 2)]
    return local_call(flatten_body, "flatten", [hidden], shapes)


def join_body(*refs):
    for i, ref in enumerate(refs[:-1]):
        refs[-1][i] = ref[...]


def join(parts):
    out_shape = jax.ShapeDtypeStruct((len(parts), *parts[0].shape), parts[0].dtype)
    return local_call(join_body, "join", parts, out_shape)


def base_body(halves, has_total, *refs):
    refs = list(refs)
    arrays = [[refs.pop(0) for _ in names] for names in halves]
    weight_ref = refs.pop(0)
    total_ref = refs.pop(0) if has_total else None
    out_ref, chunks, blocks, sems = refs
    width = blocks.shape[1]
    half = chunks.shape[1]

    jobs = []
    for h, (names, half_refs) in enumerate(zip(halves, arrays)):
        for places, ref in zip(names, half_refs):
            for i, place in enumerate(places):
                jobs.append((h, place, ref.at[i]))
    jobs.sort(key=lambda job: job[0])

    def copies(j):
        start = pl.multiple_of(place_of(jobs[j][1]) * width, width)
        block = weight_ref.at[pl.ds(start, width)]
        return (
            pltpu.make_async_copy(jobs[j][2], chunks.at[j], sems.at[j, 0]),
            pltpu.make_async_copy(block, blocks.at[j], sems.at[j, 1]),
        )

    held = [copies(j) for j in range(len(jobs))]
    for pair in held[:AHEAD]:
        for copy in pair:
            copy.start()
    for h in range(len(halves)):
        cut = pl.ds(h * half, half)
        total = total_ref[cut, :] if has_total else None
        for j, job in enumerate(jobs):
            if job[0] != h:
                continue
            for copy in held[j]:
                copy.wait()
            for pair in held[j + AHEAD : j + AHEAD + 1]:
                for copy in pair:
                    copy.start()
            term = jnp.dot(chunks[j], blocks[j], preferred_element_type=jnp.float32)
            total = term if total is None else total + term
        if out_ref.ndim == 3:
            part = out_ref.shape[0] // len(halves)
            shape = (part, *out_ref.shape[1:])
            out_ref[pl.ds(h * part, part)] = total.astype(out_ref.dtype).reshape(shape)
        else:
            out_ref[cut, :] = total


def in_hbm(value):
    return pltpu.with_memory_space_constraint(value, pltpu.HBM)


def base_dots(halves, weights, total, last=None):
    names = [[places for _, places in half] for half in halves]
    arrays = [in_hbm(array) for half in halves for array, _ in half]
    jobs = sum(len(places) for half in names for places in half)
    rows, width = arrays[0].shape[1:]
    columns = weights.shape[1]
    totals = [] if total is None else [in_vmem(total)]
    in_place = pl.BlockSpec(memory_space=pltpu.VMEM)
    return pl.pallas_call(
        functools.partial(base_body, names, total is not None),
        in_specs=[pl.BlockSpec(memory_space=pltpu.HBM)] * (len(arrays) + 1)
        + [in_place] * len(totals),
        out_specs=in_place,
        out_shape=pltpu.VMEM((2 * rows, columns), jnp.float32) if last is None else last,
        scratch_shapes=[
            pltpu.VMEM((jobs, rows, width), arrays[0].dtype),
            pltpu.VMEM((jobs, width, columns), weights.dtype),
            pltpu.SemaphoreType.DMA((jobs, 2)),
        ],
        compiler_params=pltpu.CompilerParams(vmem_limit_bytes=VMEM_BYTES),
        cost_estimate=pl.CostEstimate(
            flops=2 * rows * width * columns * jobs, bytes_accessed=2**20, transcendentals=0
        ),
        name="base_dots",
    )(*arrays, in_hbm(weights), *totals)


def flat_pages(pages):
    return in_hbm(pages.reshape(pages.shape[0] * pages.shape[1], pages.shape[2]))


def scores_body(rank_width, slot_ref, rows_ref, pages_ref, out_ref, sum_ref):
    step = pl.program_id(0)

    @pl.when(step == 0)
    def _():
        sum_ref[...] = jnp.zeros(sum_ref.shape, sum_ref.dtype)

    scores = lax.dot_general(
        pages_ref[...],
        rows_ref[...],
        (((1,), (1,)), ((), ())),
        preferred_element_type=jnp.float32,
    )
    slot = slot_ref[...] - step * DOWN_BLOCK
    partial = sum_ref[...]
    for s in range(DOWN_BLOCK):
        part = scores[s * rank_width : (s + 1) * rank_width]
        partial = partial + jnp.where(slot == s, part, 0.0)
    sum_ref[...] = partial

    @pl.when(step == pl.num_programs(0) - 1)
    def _():
        out_ref[...] = partial.reshape(out_ref.shape)


def rank_scores(slot, rows, down, shares):
    pages, rank_width, width = down.shape
    count = rows.shape[0]
    in_place = pl.BlockSpec(memory_space=pltpu.VMEM)
    return pl.pallas_call(
        functools.partial(scores_body, rank_width),
        grid=(pages // DOWN_BLOCK,),
        in_specs=[
            in_place,
            in_place,
            pl.BlockSpec((DOWN_BLOCK * rank_width, width), lambda i: (i, 0)),
        ],
        out_specs=in_place,
        out_shape=jax.ShapeDtypeStruct((shares, rank_width // shares, count), jnp.float32),
        scratch_shapes=[pltpu.VMEM((rank_width, count), jnp.float32)],
        compiler_params=pltpu.CompilerParams(vmem_limit_bytes=VMEM_BYTES),
        cost_estimate=pl.CostEstimate(
            flops=2 * count * width * pages * rank_width, bytes_accessed=5 * 2**20, transcendentals=0
        ),
        name="rank_scores",
    )(in_vmem(slot), in_vmem(rows), flat_pages(down))


def reduce_body(parts_ref, rank_ref, out_ref):
    shares, share, count = parts_ref.shape
    rank_sum = jnp.sum(parts_ref[...], axis=0)
    rank = rank_ref[...]
    own = lax.axis_index("tp") * share + lax.broadcasted_iota(jnp.int32, (share, count), 0)
    scale = 32.0 / rank.astype(jnp.float32)
    reduced = jnp.where(own < rank, rank_sum * scale, 0.0).astype(out_ref.dtype)
    out_ref[...] = jnp.broadcast_to(reduced[None], out_ref.shape)


def reduce_ranks(parts, rank):
    return local_call(
        reduce_body, "reduce_ranks", [parts, rank], jax.ShapeDtypeStruct(parts.shape, jnp.bfloat16)
    )


def up_body(rank_width, slot_ref, reduced_ref, pages_ref, total_ref, out_ref, lora_ref, pair_ref):
    step = pl.program_id(0)

    @pl.when(step == 0)
    def _():
        reduced = reduced_ref[...].astype(jnp.float32).reshape(rank_width, -1)
        pair_ref[...] = jnp.concatenate([reduced, reduced], axis=0).T.astype(pair_ref.dtype)

    lane_slot = lax.broadcasted_iota(jnp.int32, pair_ref.shape, 1) // rank_width
    slot = slot_ref[...] - step * UP_BLOCK - lane_slot
    reduced = pair_ref[...]
    zero = jnp.zeros((), reduced.dtype)
    spread = jnp.concatenate(
        [jnp.where(slot == s, reduced, zero) for s in range(0, UP_BLOCK, 2)], axis=1
    )
    part = jnp.dot(spread, pages_ref[...], preferred_element_type=jnp.float32)

    @pl.when(step == 0)
    def _():
        lora_ref[...] = part

    @pl.when((step > 0) & (step < pl.num_programs(0) - 1))
    def _():
        lora_ref[...] += part

    @pl.when(step == pl.num_programs(0) - 1)
    def _():
        lora = lora_ref[...] + part
        out_ref[...] = total_ref[...] + lora.astype(jnp.bfloat16).astype(jnp.float32)


def add_lora(slot, reduced, up, total):
    pages, rank_width, width = up.shape
    count = total.shape[0]
    in_place = pl.BlockSpec(memory_space=pltpu.VMEM)
    return pl.pallas_call(
        functools.partial(up_body, rank_width),
        grid=(pages // UP_BLOCK,),
        in_specs=[
            in_place,
            in_place,
            pl.BlockSpec((UP_BLOCK * rank_width, width), lambda i: (i, 0)),
            in_place,
        ],
        out_specs=in_place,
        out_shape=pltpu.VMEM((count, width), jnp.float32),
        scratch_shapes=[
            pltpu.VMEM((count, width), jnp.float32),
            pltpu.VMEM((count, 2 * rank_width), jnp.bfloat16),
        ],
        compiler_params=pltpu.CompilerParams(vmem_limit_bytes=VMEM_BYTES),
        cost_estimate=pl.CostEstimate(
            flops=2 * count * width * pages * rank_width, bytes_accessed=8 * 2**20, transcendentals=0
        ),
        name="add_lora",
    )(in_vmem(slot), in_vmem(reduced), flat_pages(up), in_vmem(total))


def lookup(table, index):
    onehot = index[:, None] == jnp.arange(table.shape[0], dtype=jnp.int32)[None, :]
    return jnp.sum(jnp.where(onehot, table[None, :], 0), axis=1)


def per_device(
    hidden_inputs, base_matrix, adapter_down, adapter_up, adapter_ranks, adapter_pages, row_adapters
):
    row_count, steps, width = hidden_inputs.shape
    flat_count = row_count * steps
    tp_size = SIDE * SIDE

    rows, first, second = flatten(hidden_inputs)
    down = lax.all_gather(adapter_down, "group", axis=0, tiled=True)
    up = lax.all_gather(after(adapter_up, adapter_down), "group", axis=0, tiled=True)
    slot = jnp.repeat(lookup(adapter_pages, row_adapters), steps)
    rank = jnp.repeat(lookup(adapter_ranks, row_adapters), steps)

    send = Messages().send
    first_1 = send(first, 1, 0)
    second_1 = send(second, 0, 1)
    first_3 = send(first, -1, 0)
    second_3 = send(second, 0, -1)
    first_2 = send(first_1, 1, 0)
    second_2 = send(second_1, 0, 1)
    line = (0, 1, -1, 2)
    first_line = join([first, first_1, first_3, first_2])
    second_line = join([second, second_1, second_3, second_2])

    def both(first_part, second_part, step):
        return [
            [(first_part, [(along, step) for along in line])],
            [(second_part, [(step, along) for along in line])],
        ]

    first_ahead = send(first_line, 0, 1)
    second_ahead = send(second_line, 1, 0)
    total = base_dots(both(first_line, second_line, 0), base_matrix, None)
    first_back = send(first_line, 0, -1, waits=[total])
    second_back = send(second_line, -1, 0)
    partial = rank_scores(slot[None, :], rows, down, tp_size)
    parts = lax.all_to_all(partial, "tp", 0, 0, tiled=True)
    first_far = send(first_ahead, 0, 1, waits=[parts])
    second_far = send(second_ahead, 1, 0)
    reduced = lax.all_to_all(reduce_ranks(parts, rank[None, :]), "tp", 0, 0, tiled=True)
    total = base_dots(both(first_ahead, second_ahead, 1), base_matrix, total)
    total = base_dots(both(first_back, second_back, -1), base_matrix, total)
    total = add_lora(slot[:, None], reduced, up, total)
    last = jax.ShapeDtypeStruct(hidden_inputs.shape, hidden_inputs.dtype)
    return base_dots(both(first_far, second_far, 2), base_matrix, total, last)


def solution(mesh):
    return jax.shard_map(
        per_device,
        mesh=mesh,
        in_specs=(
            P("group", None, "tp"),
            P(None, "tp"),
            P("group", None, "tp"),
            P("group", None, "tp"),
            P(),
            P(),
            P("group"),
        ),
        out_specs=P("group", None, "tp"),
        check_vma=False,
    )
```

time: 289 us -> 118 us (0.41)
  waiting for transfers between devices: 245 us -> 37.6 us
  Pallas kernels: 0 us -> 33.7 us
  starting transfers between devices: 0.12 us -> 27.9 us
  matrix products: 24.3 us -> 0 us
    all_gather x3 -> x2, waiting for transfers between devices: 161 us -> 0.02 us  [the longest x1 0.02 us: per_device(): lax.all_gather(after(adapter_up, adapter_down), 'group', axis=0, tiled=True)]
    psum x1 -> x0, waiting for transfers between devices: 83.2 us -> none  [adapter_apply(): rank_sum = lax.psum(partial_sum, 'tp')]
    pallas_call x0 -> x10, Pallas kernels: none -> 33.7 us  [the longest x4 19.5 us: base_dots(): pl.pallas_call(functools.partial(base_body, names, total is not None), in...]
    ppermute x0 -> x12, waiting for transfers between devices: none -> 24.9 us  [shift(): return lax.ppermute(value, BOTH, shift_pairs(dx, dy))]
    dot_general x3 -> x0, matrix products: 24.3 us -> none  [the longest x1 12 us: per_device(): jnp.dot(flat_rows, base_matrix, preferred_element_type=jnp.float32)]
    all_to_all x0 -> x2, starting transfers between devices: none -> 14.9 us  [the longest x1 8.34 us: per_device(): lax.all_to_all(reduce_ranks(parts, rank[None, :]), 'tp', 0, 0, tiled=True)]
    ppermute x0 -> x12, starting transfers between devices: none -> 12.9 us  [shift(): return lax.ppermute(value, BOTH, shift_pairs(dx, dy))]
    all_to_all x0 -> x2, waiting for transfers between devices: none -> 11.3 us  [the longest x1 6.75 us: per_device(): parts = lax.all_to_all(partial, 'tp', 0, 0, tiled=True)]
  transfers between devices with their start and end apart: 4 -> 16, of which waited for: 4 -> 7; matrix products, arithmetic and copies ran while one was open for 3% -> 1% of each run, Pallas kernels for 0% -> 24%
where the time goes in v2:
time: 118 us; the launch traced here: 116 us
  waiting for transfers between devices  37.6 us (32%)
  Pallas kernels  33.7 us (29%)
  starting transfers between devices  27.9 us (24%)
  between operations  13.6 us (12%)
  local copies, waits for them, and re-layouts  3.44 us (3%)
    ppermute x12, waiting for transfers between devices, shift(): return lax.ppermute(value, BOTH, shift_pairs(dx, dy))  24.9 us
    pallas_call x4, Pallas kernels, base_dots(): pl.pallas_call(functools.partial(base_body, names, total is not None), in...  19.5 us
    ppermute x12, starting transfers between devices, shift(): return lax.ppermute(value, BOTH, shift_pairs(dx, dy))  12.9 us
    all_to_all x1, starting transfers between devices, per_device(): lax.all_to_all(reduce_ranks(parts, rank[None, :]), 'tp', 0, 0, tiled=True)  8.34 us
    all_to_all x1, waiting for transfers between devices, per_device(): parts = lax.all_to_all(partial, 'tp', 0, 0, tiled=True)  6.75 us
    all_to_all x1, starting transfers between devices, per_device(): parts = lax.all_to_all(partial, 'tp', 0, 0, tiled=True)  6.54 us
    pallas_call x1, Pallas kernels, rank_scores(): pl.pallas_call(functools.partial(scores_body, rank_width), grid=(pages //...  6.27 us
    pallas_call x1, Pallas kernels, add_lora(): pl.pallas_call(functools.partial(up_body, rank_width), grid=(pages // UP_...  5.7 us
  transfers between devices with their start and end apart: 16, of which 7 were waited for; matrix products, arithmetic and copies ran while one was open for 1% of the time, Pallas kernels for 24%

profile of v2, /device:TPU:102, one launch (start us, length us, event | category | flops | bytes accessed | tf_op | source)
XLA Modules:
  0.0 116.3 jit_solution(3598421909941455799)
XLA Ops:
  6.5 0.7 all-gather.3.cloned.1.call-update
  7.3 0.0 all-gather.5.cloned.1.call-start
  7.3 0.7 all-gather.5.cloned.1.call-update
  8.0 0.2 flatten.1
  8.2 0.0 copy-start.3
  8.2 0.9 copy-done.3
  9.1 1.6 %collective-permute-start.5 = (bf16[384,512]{1,0:T(8,128)(2,1)S(1)}, bf16[384,512]{1,0:T(8,128)(2,1)S(1)}, u32[]{:S(2)}, u32[]{:S(2)}) collective-permute-start(bf16[384,512]{1,0:T(8,128)(2,1)S(1)} %get-tuple-element.22.refs_0_), channel_id=1, source_target_pairs={{0,1},{1,2},{2,3},{3,0},{4,5},{5,6},{6,7},{7,4},{8,9},{9,10},{10,1... | collective-permute-start | bytes 1179656 | tf_op jit(solution)/shard_map/ppermute | solution.py:31
  10.6 0.5 collective-permute-start
  11.1 1.7 %collective-permute-start.6 = (bf16[384,512]{1,0:T(8,128)(2,1)S(1)}, bf16[384,512]{1,0:T(8,128)(2,1)S(1)}, u32[]{:S(2)}, u32[]{:S(2)}) collective-permute-start(bf16[384,512]{1,0:T(8,128)(2,1)S(1)} %get-tuple-element.22.refs_0_), channel_id=1, source_target_pairs={{0,3},{1,0},{2,1},{3,2},{4,7},{5,4},{6,5},{7,6},{8,11},{9,8},{10,9... | collective-permute-start | bytes 1179656 | tf_op jit(solution)/shard_map/ppermute | solution.py:31
  12.8 5.3 %collective-permute-done.5.refs_1_ = bf16[384,512]{1,0:T(8,128)(2,1)S(1)} collective-permute-done((bf16[384,512]{1,0:T(8,128)(2,1)S(1)}, bf16[384,512]{1,0:T(8,128)(2,1)S(1)}, u32[]{:S(2)}, u32[]{:S(2)}) %collective-permute-start.5) | collective-permute-done | bytes 393248 | tf_op jit(solution)/shard_map/ppermute | solution.py:31
  18.0 0.4 collective-permute-start.7
  18.4 0.8 collective-permute-start.1
  19.2 2.9 %collective-permute-done.refs_1_ = bf16[384,512]{1,0:T(8,128)(2,1)S(1)} collective-permute-done((bf16[384,512]{1,0:T(8,128)(2,1)S(1)}, bf16[384,512]{1,0:T(8,128)(2,1)S(1)}, u32[]{:S(2)}, u32[]{:S(2)}) %collective-permute-start) | collective-permute-done | bytes 393248 | tf_op jit(solution)/shard_map/ppermute | solution.py:31
  22.1 0.0 collective-permute-start.2
  22.1 0.0 collective-permute-done.6.refs_2_
  22.1 7.2 %collective-permute-done.7.refs_3_ = bf16[384,512]{1,0:T(8,128)(2,1)S(1)} collective-permute-done((bf16[384,512]{1,0:T(8,128)(2,1)S(1)}, bf16[384,512]{1,0:T(8,128)(2,1)S(1)}, u32[]{:S(2)}, u32[]{:S(2)}) %collective-permute-start.7) | collective-permute-done | bytes 393248 | tf_op jit(solution)/shard_map/ppermute | solution.py:31
  29.3 0.1 join.3.refs_1_
  29.4 0.0 copy-start.5
  29.5 0.0 copy-start.6
  29.5 0.0 copy-start.7
  29.5 2.0 %collective-permute-start.8 = (bf16[4,384,512]{2,1,0:T(8,128)(2,1)S(1)}, bf16[4,384,512]{2,1,0:T(8,128)(2,1)}, u32[]{:S(2)}, u32[]{:S(2)}) collective-permute-start(bf16[4,384,512]{2,1,0:T(8,128)(2,1)S(1)} %join.3.refs_1_), channel_id=1, source_target_pairs={{0,4},{1,5},{2,6},{3,7},{4,8},{5,9},{6,10},{7,11},{8,12},{9,13},{1... | collective-permute-start | bytes 4718600 | tf_op jit(solution)/shard_map/ppermute | solution.py:31
  31.5 0.0 collective-permute-done.1.refs_2_
  31.5 1.2 %join.2.refs_0_ = bf16[4,384,512]{2,1,0:T(8,128)(2,1)} custom-call(bf16[384,512]{1,0:T(8,128)(2,1)S(1)} %get-tuple-element.17.refs_0_, bf16[384,512]{1,0:T(8,128)(2,1)S(1)} %collective-permute-done.refs_1_, bf16[384,512]{1,0:T(8,128)(2,1)S(1)} %collective-permute-done.1.refs_2_, bf16[384,512]{1,0:T(8,128)(2,1)S(1)} %collective-permute-done.2.refs_3_), custom_call_target="tpu_custom_call" | custom-call | bytes 1048576 | tf_op jit(solution)/shard_map/join/pallas_call | solution.py:63
  32.7 0.1 select_reduce_fusion
  32.8 0.1 broadcast_in_dim.32
  32.9 0.2 broadcast_in_dim_reshape.9.slot_ref
  33.1 4.6 %base_dots.4.refs_3_ = f32[768,512]{1,0:T(8,128)S(1)} custom-call(bf16[4,384,512]{2,1,0:T(8,128)(2,1)} %join.2.refs_0_, bf16[4,384,512]{2,1,0:T(8,128)(2,1)} %copy-done, bf16[8192,512]{1,0:T(8,128)(2,1)} %refs_2_.7), custom_call_target="tpu_custom_call" | custom-call | flops 1610612736 | bytes 1048576 | tf_op jit(solution)/shard_map/base_dots/pallas_call | solution.py:161
  37.8 3.3 %collective-permute-start.10 = (bf16[4,384,512]{2,1,0:T(8,128)(2,1)}, bf16[4,384,512]{2,1,0:T(8,128)(2,1)}, u32[]{:S(2)}, u32[]{:S(2)}) collective-permute-start(bf16[4,384,512]{2,1,0:T(8,128)(2,1)} %join.2.refs_0_), channel_id=1, source_target_pairs={{0,3},{1,0},{2,1},{3,2},{4,7},{5,4},{6,5},{7,6},{8,11},{9,8},{10,9... | collective-permute-start | bytes 4718600 | tf_op jit(solution)/shard_map/ppermute | solution.py:31
  41.1 0.1 collective-permute-start.11
  41.2 1.1 copy-done.4
  42.3 6.3 %rank_scores.1 = f32[16,4,768]{2,1,0:T(4,128)} custom-call(s32[1,768]{1,0:T(1,128)S(1)} %broadcast_in_dim_reshape.9.slot_ref, bf16[768,512]{1,0:T(8,128)(2,1)S(1)} %copy-done.4, bf16[4096,512]{1,0:T(8,128)(2,1)} %bitcast.3), custom_call_target="tpu_custom_call" | custom-call | flops 3221225472 | bytes 5242880 | tf_op jit(solution)/shard_map/rank_scores/pallas_call | solution.py:213
  48.6 6.5 %all-to-all-start = ((f32[16,4,768]{2,1,0:T(4,128)}), f32[16,4,768]{2,1,0:T(4,128)S(1)}, u32[]{:S(2)}, u32[]{:S(2)}) async-start(f32[16,4,768]{2,1,0:T(4,128)} %rank_scores.1), calls=%async_computation | async-start | bytes 393216 | tf_op jit(solution)/shard_map/all_to_all | solution.py:347
  55.2 5.4 %collective-permute-done.8.refs_1_ = bf16[4,384,512]{2,1,0:T(8,128)(2,1)} collective-permute-done((bf16[4,384,512]{2,1,0:T(8,128)(2,1)S(1)}, bf16[4,384,512]{2,1,0:T(8,128)(2,1)}, u32[]{:S(2)}, u32[]{:S(2)}) %collective-permute-start.8) | collective-permute-done | bytes 1572896 | tf_op jit(solution)/shard_map/ppermute | solution.py:31
  60.6 2.1 %collective-permute-start.9 = (bf16[4,384,512]{2,1,0:T(8,128)(2,1)}, bf16[4,384,512]{2,1,0:T(8,128)(2,1)}, u32[]{:S(2)}, u32[]{:S(2)}) collective-permute-start(bf16[4,384,512]{2,1,0:T(8,128)(2,1)} %collective-permute-done.8.refs_1_), channel_id=1, source_target_pairs={{0,4},{1,5},{2,6},{3,7},{4,8},{5,9},{6,10},{7,11},{8,12},{9,13},{1... | collective-permute-start | bytes 4718600 | tf_op jit(solution)/shard_map/ppermute | solution.py:31
  62.7 4.1 %collective-permute-done.3.refs_0_ = bf16[4,384,512]{2,1,0:T(8,128)(2,1)} collective-permute-done((bf16[4,384,512]{2,1,0:T(8,128)(2,1)}, bf16[4,384,512]{2,1,0:T(8,128)(2,1)}, u32[]{:S(2)}, u32[]{:S(2)}) %collective-permute-start.3) | collective-permute-done | bytes 1572896 | tf_op jit(solution)/shard_map/ppermute | solution.py:31
  66.9 6.8 %all-to-all-done.parts_ref = f32[16,4,768]{2,1,0:T(4,128)S(1)} async-done(((f32[16,4,768]{2,1,0:T(4,128)}), f32[16,4,768]{2,1,0:T(4,128)S(1)}, u32[]{:S(2)}, u32[]{:S(2)}) %all-to-all-start) | async-done | bytes 196640 | tf_op jit(solution)/shard_map/all_to_all | solution.py:347
  73.6 0.4 collective-permute-start.4
  74.1 0.9 broadcast_in_dim_reshape.12.slot_ref
  74.9 0.1 broadcast_in_dim.34
  75.0 0.2 broadcast_in_dim_reshape.11.rank_ref
  75.2 4.7 %base_dots.5.refs_3_ = f32[768,512]{1,0:T(8,128)S(1)} custom-call(bf16[4,384,512]{2,1,0:T(8,128)(2,1)} %collective-permute-done.3.refs_0_, bf16[4,384,512]{2,1,0:T(8,128)(2,1)} %collective-permute-done.8.refs_1_, bf16[8192,512]{1,0:T(8,128)(2,1)} %refs_2_.7, f32[768,512]{1,0:T(8,128)S(1)} %base_dots.4.refs_3_), custom_call_target="tpu_custom_call" | custom-call | flops 1610612736 | bytes 1048576 | tf_op jit(solution)/shard_map/base_dots/pallas_call | solution.py:161
  79.9 0.7 reduce_ranks.1
  80.5 8.3 %all-to-all-start.1 = ((bf16[16,4,768]{2,1,0:T(4,128)(2,1)}), bf16[16,4,768]{2,1,0:T(4,128)(2,1)}, u32[]{:S(2)}, u32[]{:S(2)}) async-start(bf16[16,4,768]{2,1,0:T(4,128)(2,1)} %reduce_ranks.1), calls=%async_computation.1 | async-start | bytes 196608 | tf_op jit(solution)/shard_map/all_to_all | solution.py:350
  88.9 4.7 %base_dots.6.total_ref = f32[768,512]{1,0:T(8,128)S(1)} custom-call(bf16[4,384,512]{2,1,0:T(8,128)(2,1)} %collective-permute-done.10.refs_0_, bf16[4,384,512]{2,1,0:T(8,128)(2,1)} %collective-permute-done.11.refs_1_, bf16[8192,512]{1,0:T(8,128)(2,1)} %refs_2_.7, f32[768,512]{1,0:T(8,128)S(1)} %base_dots.5.refs_3_), custom_call_target="tpu_custom_call" | custom-call | flops 1610612736 | bytes 1048576 | tf_op jit(solution)/shard_map/base_dots/pallas_call | solution.py:161
  93.6 0.0 all-gather.5.cloned.1.call-done
  93.6 4.5 %all-to-all-done.1.reduced_ref = bf16[16,4,768]{2,1,0:T(4,128)(2,1)} async-done(((bf16[16,4,768]{2,1,0:T(4,128)(2,1)}), bf16[16,4,768]{2,1,0:T(4,128)(2,1)}, u32[]{:S(2)}, u32[]{:S(2)}) %all-to-all-start.1) | async-done | bytes 98336 | tf_op jit(solution)/shard_map/all_to_all | solution.py:350
  98.1 5.7 %add_lora.1.refs_3_ = f32[768,512]{1,0:T(8,128)S(1)} custom-call(s32[768,1]{1,0:T(8,128)S(1)} %copy-done.2, bf16[16,4,768]{2,1,0:T(4,128)(2,1)} %all-to-all-done.1.reduced_ref, bf16[4096,512]{1,0:T(8,128)(2,1)} %bitcast.2, f32[768,512]{1,0:T(8,128)S(1)} %base_dots.6.total_ref), custom_call_target="tpu_custom_call" | custom-call | flops 3221225472 | bytes 8388608 | tf_op jit(solution)/shard_map/add_lora/pallas_call | solution.py:283
  103.9 5.5 %base_dots.7 = bf16[384,2,512]{2,1,0:T(2,128)(2,1)} custom-call(bf16[4,384,512]{2,1,0:T(8,128)(2,1)} %collective-permute-done.4.refs_0_, bf16[4,384,512]{2,1,0:T(8,128)(2,1)} %collective-permute-done.9.refs_1_, bf16[8192,512]{1,0:T(8,128)(2,1)} %refs_2_.7, f32[768,512]{1,0:T(8,128)S(1)} %add_lora.1.refs_3_), custom_call_target="tpu_custom_call" | custom-call | flops 1610612736 | bytes 1048576 | tf_op jit(solution)/shard_map/base_dots/pallas_call | solution.py:161
  (18 shorter events, 0.0 us)
Async XLA Ops:
  6.5 1.5 %copy-start.1 = (bf16[384,2,512]{2,1,0:T(2,128)(2,1)S(1)}, bf16[384,2,512]{2,1,0:T(2,128)(2,1)}, u32[]{:S(2)}) copy-start(bf16[384,2,512]{2,1,0:T(2,128)(2,1)} %hidden_ref.1) | copy-start | bytes 2359300
  6.5 34.7 %all-gather.3.cloned.1.call-start = ((), (), s32[]{:S(2)}) async-start(), calls=%async_computation.2 | async-start | bytes 4718592 | tf_op jit(solution)/shard_map/all_gather | solution.py:319
  7.3 86.4 %all-gather.5.cloned.1.call-start = ((), (), s32[]{:S(2)}) async-start(), calls=%async_computation.3 | async-start | bytes 4718592 | tf_op jit(solution)/shard_map/all_gather | solution.py:320
  8.2 0.9 copy-start.3
  9.1 9.0 %collective-permute-start.5 = (bf16[384,512]{1,0:T(8,128)(2,1)S(1)}, bf16[384,512]{1,0:T(8,128)(2,1)S(1)}, u32[]{:S(2)}, u32[]{:S(2)}) collective-permute-start(bf16[384,512]{1,0:T(8,128)(2,1)S(1)} %get-tuple-element.22.refs_0_), channel_id=1, source_target_pairs={{0,1},{1,2},{2,3},{3,0},{4,5},{5,6},{6,7},{7,4},{8,9},{9,10},{10,1... | collective-permute-start | bytes 1179656 | tf_op jit(solution)/shard_map/ppermute | solution.py:31
  10.6 11.5 %collective-permute-start = (bf16[384,512]{1,0:T(8,128)(2,1)S(1)}, bf16[384,512]{1,0:T(8,128)(2,1)S(1)}, u32[]{:S(2)}, u32[]{:S(2)}) collective-permute-start(bf16[384,512]{1,0:T(8,128)(2,1)S(1)} %get-tuple-element.17.refs_0_), channel_id=1, source_target_pairs={{0,4},{1,5},{2,6},{3,7},{4,8},{5,9},{6,10},{7,11},{8,12},{9,13},{1... | collective-permute-start | bytes 1179656 | tf_op jit(solution)/shard_map/ppermute | solution.py:31
  11.1 11.0 %collective-permute-start.6 = (bf16[384,512]{1,0:T(8,128)(2,1)S(1)}, bf16[384,512]{1,0:T(8,128)(2,1)S(1)}, u32[]{:S(2)}, u32[]{:S(2)}) collective-permute-start(bf16[384,512]{1,0:T(8,128)(2,1)S(1)} %get-tuple-element.22.refs_0_), channel_id=1, source_target_pairs={{0,3},{1,0},{2,1},{3,2},{4,7},{5,4},{6,5},{7,6},{8,11},{9,8},{10,9... | collective-permute-start | bytes 1179656 | tf_op jit(solution)/shard_map/ppermute | solution.py:31
  18.0 11.3 %collective-permute-start.7 = (bf16[384,512]{1,0:T(8,128)(2,1)S(1)}, bf16[384,512]{1,0:T(8,128)(2,1)S(1)}, u32[]{:S(2)}, u32[]{:S(2)}) collective-permute-start(bf16[384,512]{1,0:T(8,128)(2,1)S(1)} %collective-permute-done.5.refs_1_), channel_id=1, source_target_pairs={{0,1},{1,2},{2,3},{3,0},{4,5},{5,6},{6,7},{7,4},{8,9},{9,10},{10,1... | collective-permute-start | bytes 1179656 | tf_op jit(solution)/shard_map/ppermute | solution.py:31
  18.4 13.0 %collective-permute-start.1 = (bf16[384,512]{1,0:T(8,128)(2,1)S(1)}, bf16[384,512]{1,0:T(8,128)(2,1)S(1)}, u32[]{:S(2)}, u32[]{:S(2)}) collective-permute-start(bf16[384,512]{1,0:T(8,128)(2,1)S(1)} %get-tuple-element.17.refs_0_), channel_id=1, source_target_pairs={{0,12},{1,13},{2,14},{3,15},{4,0},{5,1},{6,2},{7,3},{8,4},{9,5},{1... | collective-permute-start | bytes 1179656 | tf_op jit(solution)/shard_map/ppermute | solution.py:31
  22.1 9.4 %collective-permute-start.2 = (bf16[384,512]{1,0:T(8,128)(2,1)S(1)}, bf16[384,512]{1,0:T(8,128)(2,1)S(1)}, u32[]{:S(2)}, u32[]{:S(2)}) collective-permute-start(bf16[384,512]{1,0:T(8,128)(2,1)S(1)} %collective-permute-done.refs_1_), channel_id=1, source_target_pairs={{0,4},{1,5},{2,6},{3,7},{4,8},{5,9},{6,10},{7,11},{8,12},{9,13},{1... | collective-permute-start | bytes 1179656 | tf_op jit(solution)/shard_map/ppermute | solution.py:31
  29.4 3.7 %copy-start = (bf16[4,384,512]{2,1,0:T(8,128)(2,1)}, bf16[4,384,512]{2,1,0:T(8,128)(2,1)S(1)}, u32[]{:S(2)}) copy-start(bf16[4,384,512]{2,1,0:T(8,128)(2,1)S(1)} %join.3.refs_1_) | copy-start | bytes 4718596
  29.4 3.3 %copy-start.5 = (s32[384]{0:T(512)S(1)}, s32[384]{0:T(512)}, u32[]{:S(2)}) copy-start(s32[384]{0:T(512)} %param.13) | copy-start | bytes 4612
  29.5 3.3 %copy-start.6 = (s32[64]{0:T(128)S(1)}, s32[64]{0:T(128)}, u32[]{:S(2)}) copy-start(s32[64]{0:T(128)} %param.11) | copy-start | bytes 772
  29.5 3.3 %copy-start.7 = (s32[64]{0:T(128)S(1)}, s32[64]{0:T(128)}, u32[]{:S(2)}) copy-start(s32[64]{0:T(128)} %param.12) | copy-start | bytes 772
  29.5 31.1 %collective-permute-start.8 = (bf16[4,384,512]{2,1,0:T(8,128)(2,1)S(1)}, bf16[4,384,512]{2,1,0:T(8,128)(2,1)}, u32[]{:S(2)}, u32[]{:S(2)}) collective-permute-start(bf16[4,384,512]{2,1,0:T(8,128)(2,1)S(1)} %join.3.refs_1_), channel_id=1, source_target_pairs={{0,4},{1,5},{2,6},{3,7},{4,8},{5,9},{6,10},{7,11},{8,12},{9,13},{1... | collective-permute-start | bytes 4718600 | tf_op jit(solution)/shard_map/ppermute | solution.py:31
  32.7 34.1 %collective-permute-start.3 = (bf16[4,384,512]{2,1,0:T(8,128)(2,1)}, bf16[4,384,512]{2,1,0:T(8,128)(2,1)}, u32[]{:S(2)}, u32[]{:S(2)}) collective-permute-start(bf16[4,384,512]{2,1,0:T(8,128)(2,1)} %join.2.refs_0_), channel_id=1, source_target_pairs={{0,1},{1,2},{2,3},{3,0},{4,5},{5,6},{6,7},{7,4},{8,9},{9,10},{10,1... | collective-permute-start | bytes 4718600 | tf_op jit(solution)/shard_map/ppermute | solution.py:31
  37.8 51.1 %collective-permute-start.10 = (bf16[4,384,512]{2,1,0:T(8,128)(2,1)}, bf16[4,384,512]{2,1,0:T(8,128)(2,1)}, u32[]{:S(2)}, u32[]{:S(2)}) collective-permute-start(bf16[4,384,512]{2,1,0:T(8,128)(2,1)} %join.2.refs_0_), channel_id=1, source_target_pairs={{0,3},{1,0},{2,1},{3,2},{4,7},{5,4},{6,5},{7,6},{8,11},{9,8},{10,9... | collective-permute-start | bytes 4718600 | tf_op jit(solution)/shard_map/ppermute | solution.py:31
  41.1 47.8 %collective-permute-start.11 = (bf16[4,384,512]{2,1,0:T(8,128)(2,1)}, bf16[4,384,512]{2,1,0:T(8,128)(2,1)}, u32[]{:S(2)}, u32[]{:S(2)}) collective-permute-start(bf16[4,384,512]{2,1,0:T(8,128)(2,1)} %copy-done), channel_id=1, source_target_pairs={{0,12},{1,13},{2,14},{3,15},{4,0},{5,1},{6,2},{7,3},{8,4},{9,5},{1... | collective-permute-start | bytes 4718600 | tf_op jit(solution)/shard_map/ppermute | solution.py:31
  41.2 1.1 copy-start.4
  48.6 25.0 %all-to-all-start = ((f32[16,4,768]{2,1,0:T(4,128)}), f32[16,4,768]{2,1,0:T(4,128)S(1)}, u32[]{:S(2)}, u32[]{:S(2)}) async-start(f32[16,4,768]{2,1,0:T(4,128)} %rank_scores.1), calls=%async_computation | async-start | bytes 393216 | tf_op jit(solution)/shard_map/all_to_all | solution.py:347
  60.6 43.3 %collective-permute-start.9 = (bf16[4,384,512]{2,1,0:T(8,128)(2,1)}, bf16[4,384,512]{2,1,0:T(8,128)(2,1)}, u32[]{:S(2)}, u32[]{:S(2)}) collective-permute-start(bf16[4,384,512]{2,1,0:T(8,128)(2,1)} %collective-permute-done.8.refs_1_), channel_id=1, source_target_pairs={{0,4},{1,5},{2,6},{3,7},{4,8},{5,9},{6,10},{7,11},{8,12},{9,13},{1... | collective-permute-start | bytes 4718600 | tf_op jit(solution)/shard_map/ppermute | solution.py:31
  73.6 30.3 %collective-permute-start.4 = (bf16[4,384,512]{2,1,0:T(8,128)(2,1)}, bf16[4,384,512]{2,1,0:T(8,128)(2,1)}, u32[]{:S(2)}, u32[]{:S(2)}) collective-permute-start(bf16[4,384,512]{2,1,0:T(8,128)(2,1)} %collective-permute-done.3.refs_0_), channel_id=1, source_target_pairs={{0,1},{1,2},{2,3},{3,0},{4,5},{5,6},{6,7},{7,4},{8,9},{9,10},{10,1... | collective-permute-start | bytes 4718600 | tf_op jit(solution)/shard_map/ppermute | solution.py:31
  80.5 17.6 %all-to-all-start.1 = ((bf16[16,4,768]{2,1,0:T(4,128)(2,1)}), bf16[16,4,768]{2,1,0:T(4,128)(2,1)}, u32[]{:S(2)}, u32[]{:S(2)}) async-start(bf16[16,4,768]{2,1,0:T(4,128)(2,1)} %reduce_ranks.1), calls=%async_computation.1 | async-start | bytes 196608 | tf_op jit(solution)/shard_map/all_to_all | solution.py:350
  88.9 9.3 %copy-start.2 = (s32[768,1]{1,0:T(8,128)S(1)}, s32[768,1]{1,0:T(8,128)}, u32[]{:S(2)}) copy-start(s32[768,1]{1,0:T(8,128)} %broadcast_in_dim_reshape.12.slot_ref) | copy-start | bytes 9220
Sparse Core Ops, SparseCore 0:
  9.1 31.3 all-gather.2
  42.2 32.1 all-gather.4

commit v3 on v2

--- a/solution.py
+++ b/solution.py
@@ -12,7 +12,7 @@
 VMEM_BYTES = 28 * 2**20
 DOWN_BLOCK = 16
 UP_BLOCK = 32
-AHEAD = 3
+AHEAD = 6
 WINDOW = 4
 
 
@@ -215,7 +215,7 @@
         grid=(pages // DOWN_BLOCK,),
         in_specs=[
             in_place,
-            in_place,
+            pl.BlockSpec((count, width), lambda i: (0, 0)),
             pl.BlockSpec((DOWN_BLOCK * rank_width, width), lambda i: (i, 0)),
         ],
         out_specs=in_place,
@@ -226,7 +226,7 @@
             flops=2 * count * width * pages * rank_width, bytes_accessed=5 * 2**20, transcendentals=0
         ),
         name="rank_scores",
-    )(in_vmem(slot), in_vmem(rows), flat_pages(down))
+    )(in_vmem(slot), in_hbm(rows), flat_pages(down))
 
 
 def reduce_body(parts_ref, rank_ref, out_ref):
@@ -245,62 +245,34 @@
     )
 
 
-def up_body(rank_width, slot_ref, reduced_ref, pages_ref, total_ref, out_ref, lora_ref, pair_ref):
-    step = pl.program_id(0)
-
-    @pl.when(step == 0)
-    def _():
-        reduced = reduced_ref[...].astype(jnp.float32).reshape(rank_width, -1)
-        pair_ref[...] = jnp.concatenate([reduced, reduced], axis=0).T.astype(pair_ref.dtype)
-
-    lane_slot = lax.broadcasted_iota(jnp.int32, pair_ref.shape, 1) // rank_width
-    slot = slot_ref[...] - step * UP_BLOCK - lane_slot
-    reduced = pair_ref[...]
-    zero = jnp.zeros((), reduced.dtype)
-    spread = jnp.concatenate(
-        [jnp.where(slot == s, reduced, zero) for s in range(0, UP_BLOCK, 2)], axis=1
-    )
-    part = jnp.dot(spread, pages_ref[...], preferred_element_type=jnp.float32)
-
-    @pl.when(step == 0)
-    def _():
-        lora_ref[...] = part
-
-    @pl.when((step > 0) & (step < pl.num_programs(0) - 1))
-    def _():
-        lora_ref[...] += part
-
-    @pl.when(step == pl.num_programs(0) - 1)
-    def _():
-        lora = lora_ref[...] + part
-        out_ref[...] = total_ref[...] + lora.astype(jnp.bfloat16).astype(jnp.float32)
+def up_body(rank_width, slot_ref, reduced_ref, pages_ref, total_ref, out_ref):
+    reduced = reduced_ref[...].astype(jnp.float32).reshape(rank_width, -1)
+    pair = jnp.concatenate([reduced, reduced], axis=0).T.astype(reduced_ref.dtype)
+    slot = slot_ref[...] - lax.broadcasted_iota(jnp.int32, pair.shape, 1) // rank_width
+    zero = jnp.zeros((), pair.dtype)
+    depth = UP_BLOCK * rank_width
+    lora = None
+    for i in range(pages_ref.shape[0] // depth):
+        first = i * UP_BLOCK
+        spread = jnp.concatenate(
+            [jnp.where(slot == first + s, pair, zero) for s in range(0, UP_BLOCK, 2)], axis=1
+        )
+        pages = pages_ref[pl.ds(i * depth, depth), :]
+        part = jnp.dot(spread, pages, preferred_element_type=jnp.float32)
+        lora = part if lora is None else lora + part
+    out_ref[...] = total_ref[...] + lora.astype(jnp.bfloat16).astype(jnp.float32)
 
 
 def add_lora(slot, reduced, up, total):
     pages, rank_width, width = up.shape
     count = total.shape[0]
-    in_place = pl.BlockSpec(memory_space=pltpu.VMEM)
-    return pl.pallas_call(
+    return local_call(
         functools.partial(up_body, rank_width),
-        grid=(pages // UP_BLOCK,),
-        in_specs=[
-            in_place,
-            in_place,
-            pl.BlockSpec((UP_BLOCK * rank_width, width), lambda i: (i, 0)),
-            in_place,
-        ],
-        out_specs=in_place,
-        out_shape=pltpu.VMEM((count, width), jnp.float32),
-        scratch_shapes=[
-            pltpu.VMEM((count, width), jnp.float32),
-            pltpu.VMEM((count, 2 * rank_width), jnp.bfloat16),
-        ],
-        compiler_params=pltpu.CompilerParams(vmem_limit_bytes=VMEM_BYTES),
-        cost_estimate=pl.CostEstimate(
-            flops=2 * count * width * pages * rank_width, bytes_accessed=8 * 2**20, transcendentals=0
-        ),
-        name="add_lora",
-    )(in_vmem(slot), in_vmem(reduced), flat_pages(up), in_vmem(total))
+        "add_lora",
+        [slot, reduced, up.reshape(pages * rank_width, width), total],
+        pltpu.VMEM((count, width), jnp.float32),
+        flops=2 * count * width * pages * rank_width,
+    )
 
 
 def lookup(table, index):
@@ -347,8 +319,9 @@
     parts = lax.all_to_all(partial, "tp", 0, 0, tiled=True)
     first_far = send(first_ahead, 0, 1, waits=[parts])
     second_far = send(second_ahead, 1, 0)
-    reduced = lax.all_to_all(reduce_ranks(parts, rank[None, :]), "tp", 0, 0, tiled=True)
-    total = base_dots(both(first_ahead, second_ahead, 1), base_matrix, total)
+    spread = reduce_ranks(parts, rank[None, :])
+    reduced = lax.all_to_all(spread, "tp", 0, 0, tiled=True)
+    total = base_dots(both(first_ahead, second_ahead, 1), base_matrix, after(total, spread))
     total = base_dots(both(first_back, second_back, -1), base_matrix, total)
     total = add_lora(slot[:, None], reduced, up, total)
     last = jax.ShapeDtypeStruct(hidden_inputs.shape, hidden_inputs.dtype)

time: 118 us -> 116 us (0.983); the launches traced: 116 us -> 116 us
  Pallas kernels: 33.7 us -> 28.7 us
  waiting for transfers between devices: 37.6 us -> 41.1 us
    pallas_call x1 -> x0, Pallas kernels: 5.7 us -> none  [add_lora(): pl.pallas_call(functools.partial(up_body, rank_width), grid=(pages // UP_...]
    pallas_call x4 -> x5, Pallas kernels: 2.18 us -> 5.67 us  [local_call(): pl.pallas_call(body, in_specs=[pl.BlockSpec(memory_space=pltpu.VMEM)] * l...]
    pallas_call x4, Pallas kernels: 19.5 us -> 16.6 us  [base_dots(): pl.pallas_call(functools.partial(base_body, names, total is not None), in...]
    all_to_all x1, waiting for transfers between devices: 4.5 us -> 6.72 us  [per_device(): reduced = lax.all_to_all(spread, 'tp', 0, 0, tiled=True)]
    ppermute x12, waiting for transfers between devices: 24.9 us -> 26.2 us  [shift(): return lax.ppermute(value, BOTH, shift_pairs(dx, dy))]
    unnamed x16 -> x14, local copies, waits for them, and re-layouts: 2.04 us -> 3.09 us
  transfers between devices with their start and end apart: 16 -> 16, of which waited for: 7 -> 7; matrix products, arithmetic and copies ran while one was open for 1% -> 1% of each run, Pallas kernels for 24% -> 21%
where the time goes in v3:
time: 116 us
  waiting for transfers between devices  41.1 us (35%)
  starting transfers between devices  28.8 us (25%)
  Pallas kernels  28.7 us (25%)
  between operations  13.6 us (12%)
  local copies, waits for them, and re-layouts  3.74 us (3%)
    ppermute x12, waiting for transfers between devices, shift(): return lax.ppermute(value, BOTH, shift_pairs(dx, dy))  26.2 us
    pallas_call x4, Pallas kernels, base_dots(): pl.pallas_call(functools.partial(base_body, names, total is not None), in...  16.6 us
    ppermute x12, starting transfers between devices, shift(): return lax.ppermute(value, BOTH, shift_pairs(dx, dy))  13.3 us
    all_to_all x1, starting transfers between devices, per_device(): reduced = lax.all_to_all(spread, 'tp', 0, 0, tiled=True)  8.33 us
    all_to_all x1, starting transfers between devices, per_device(): parts = lax.all_to_all(partial, 'tp', 0, 0, tiled=True)  7.11 us
    all_to_all x1, waiting for transfers between devices, per_device(): parts = lax.all_to_all(partial, 'tp', 0, 0, tiled=True)  6.74 us
    all_to_all x1, waiting for transfers between devices, per_device(): reduced = lax.all_to_all(spread, 'tp', 0, 0, tiled=True)  6.72 us
    pallas_call x1, Pallas kernels, rank_scores(): pl.pallas_call(functools.partial(scores_body, rank_width), grid=(pages //...  6.49 us
  transfers between devices with their start and end apart: 16, of which 7 were waited for; matrix products, arithmetic and copies ran while one was open for 1% of the time, Pallas kernels for 21%

profile of v3, /device:TPU:102, one launch (start us, length us, event | category | flops | bytes accessed | tf_op | source)
XLA Modules:
  0.0 116.1 jit_solution(7921537976123554623)
XLA Ops:
  6.5 0.7 all-gather.3.cloned.1.call-update
  7.3 0.0 all-gather.5.cloned.1.call-start
  7.3 0.7 all-gather.5.cloned.1.call-update
  8.0 0.2 flatten.1
  8.2 0.0 copy-start.3
  8.2 0.9 copy-done.3
  9.1 1.6 %collective-permute-start.5 = (bf16[384,512]{1,0:T(8,128)(2,1)S(1)}, bf16[384,512]{1,0:T(8,128)(2,1)S(1)}, u32[]{:S(2)}, u32[]{:S(2)}) collective-permute-start(bf16[384,512]{1,0:T(8,128)(2,1)S(1)} %get-tuple-element.23.refs_0_), channel_id=1, source_target_pairs={{0,1},{1,2},{2,3},{3,0},{4,5},{5,6},{6,7},{7,4},{8,9},{9,10},{10,1... | collective-permute-start | bytes 1179656 | tf_op jit(solution)/shard_map/ppermute | solution.py:31
  10.6 0.5 collective-permute-start
  11.1 1.7 %collective-permute-start.6 = (bf16[384,512]{1,0:T(8,128)(2,1)S(1)}, bf16[384,512]{1,0:T(8,128)(2,1)S(1)}, u32[]{:S(2)}, u32[]{:S(2)}) collective-permute-start(bf16[384,512]{1,0:T(8,128)(2,1)S(1)} %get-tuple-element.23.refs_0_), channel_id=1, source_target_pairs={{0,3},{1,0},{2,1},{3,2},{4,7},{5,4},{6,5},{7,6},{8,11},{9,8},{10,9... | collective-permute-start | bytes 1179656 | tf_op jit(solution)/shard_map/ppermute | solution.py:31
  12.8 5.3 %collective-permute-done.5.refs_1_ = bf16[384,512]{1,0:T(8,128)(2,1)S(1)} collective-permute-done((bf16[384,512]{1,0:T(8,128)(2,1)S(1)}, bf16[384,512]{1,0:T(8,128)(2,1)S(1)}, u32[]{:S(2)}, u32[]{:S(2)}) %collective-permute-start.5) | collective-permute-done | bytes 393248 | tf_op jit(solution)/shard_map/ppermute | solution.py:31
  18.0 0.4 collective-permute-start.7
  18.4 0.8 collective-permute-start.1
  19.2 2.9 %collective-permute-done.refs_1_ = bf16[384,512]{1,0:T(8,128)(2,1)S(1)} collective-permute-done((bf16[384,512]{1,0:T(8,128)(2,1)S(1)}, bf16[384,512]{1,0:T(8,128)(2,1)S(1)}, u32[]{:S(2)}, u32[]{:S(2)}) %collective-permute-start) | collective-permute-done | bytes 393248 | tf_op jit(solution)/shard_map/ppermute | solution.py:31
  22.1 0.0 collective-permute-start.2
  22.1 0.0 collective-permute-done.6.refs_2_
  22.1 7.2 %collective-permute-done.7.refs_3_ = bf16[384,512]{1,0:T(8,128)(2,1)S(1)} collective-permute-done((bf16[384,512]{1,0:T(8,128)(2,1)S(1)}, bf16[384,512]{1,0:T(8,128)(2,1)S(1)}, u32[]{:S(2)}, u32[]{:S(2)}) %collective-permute-start.7) | collective-permute-done | bytes 393248 | tf_op jit(solution)/shard_map/ppermute | solution.py:31
  29.3 0.1 join.3.refs_1_
  29.4 0.0 copy-start.4
  29.5 0.0 copy-start.5
  29.5 0.0 copy-start.6
  29.5 2.0 %collective-permute-start.8 = (bf16[4,384,512]{2,1,0:T(8,128)(2,1)S(1)}, bf16[4,384,512]{2,1,0:T(8,128)(2,1)}, u32[]{:S(2)}, u32[]{:S(2)}) collective-permute-start(bf16[4,384,512]{2,1,0:T(8,128)(2,1)S(1)} %join.3.refs_1_), channel_id=1, source_target_pairs={{0,4},{1,5},{2,6},{3,7},{4,8},{5,9},{6,10},{7,11},{8,12},{9,13},{1... | collective-permute-start | bytes 4718600 | tf_op jit(solution)/shard_map/ppermute | solution.py:31
  31.5 0.0 collective-permute-done.1.refs_2_
  31.5 1.2 %join.2.refs_0_ = bf16[4,384,512]{2,1,0:T(8,128)(2,1)} custom-call(bf16[384,512]{1,0:T(8,128)(2,1)S(1)} %get-tuple-element.18.refs_0_, bf16[384,512]{1,0:T(8,128)(2,1)S(1)} %collective-permute-done.refs_1_, bf16[384,512]{1,0:T(8,128)(2,1)S(1)} %collective-permute-done.1.refs_2_, bf16[384,512]{1,0:T(8,128)(2,1)S(1)} %collective-permute-done.2.refs_3_), custom_call_target="tpu_custom_call" | custom-call | bytes 1048576 | tf_op jit(solution)/shard_map/join/pallas_call | solution.py:63
  32.7 0.1 select_reduce_fusion
  32.8 0.1 broadcast_in_dim.32
  32.9 0.2 broadcast_in_dim_reshape.9.slot_ref
  33.1 4.1 %base_dots.4.refs_3_ = f32[768,512]{1,0:T(8,128)S(1)} custom-call(bf16[4,384,512]{2,1,0:T(8,128)(2,1)} %join.2.refs_0_, bf16[4,384,512]{2,1,0:T(8,128)(2,1)} %copy-done, bf16[8192,512]{1,0:T(8,128)(2,1)} %refs_2_.7), custom_call_target="tpu_custom_call" | custom-call | flops 1610612736 | bytes 1048576 | tf_op jit(solution)/shard_map/base_dots/pallas_call | solution.py:161
  37.3 3.3 %collective-permute-start.10 = (bf16[4,384,512]{2,1,0:T(8,128)(2,1)}, bf16[4,384,512]{2,1,0:T(8,128)(2,1)}, u32[]{:S(2)}, u32[]{:S(2)}) collective-permute-start(bf16[4,384,512]{2,1,0:T(8,128)(2,1)} %join.2.refs_0_), channel_id=1, source_target_pairs={{0,3},{1,0},{2,1},{3,2},{4,7},{5,4},{6,5},{7,6},{8,11},{9,8},{10,9... | collective-permute-start | bytes 4718600 | tf_op jit(solution)/shard_map/ppermute | solution.py:31
  40.5 0.1 collective-permute-start.11
  40.6 6.5 %rank_scores.1 = f32[16,4,768]{2,1,0:T(4,128)} custom-call(s32[1,768]{1,0:T(1,128)S(1)} %broadcast_in_dim_reshape.9.slot_ref, bf16[768,512]{1,0:T(8,128)(2,1)} %copy-done.3, bf16[4096,512]{1,0:T(8,128)(2,1)} %bitcast.3), custom_call_target="tpu_custom_call" | custom-call | flops 3221225472 | bytes 5242880 | tf_op jit(solution)/shard_map/rank_scores/pallas_call | solution.py:213
  47.1 7.1 %all-to-all-start = ((f32[16,4,768]{2,1,0:T(4,128)}), f32[16,4,768]{2,1,0:T(4,128)S(1)}, u32[]{:S(2)}, u32[]{:S(2)}) async-start(f32[16,4,768]{2,1,0:T(4,128)} %rank_scores.1), calls=%async_computation | async-start | bytes 393216 | tf_op jit(solution)/shard_map/all_to_all | solution.py:319
  54.2 6.7 %collective-permute-done.8.refs_1_ = bf16[4,384,512]{2,1,0:T(8,128)(2,1)} collective-permute-done((bf16[4,384,512]{2,1,0:T(8,128)(2,1)S(1)}, bf16[4,384,512]{2,1,0:T(8,128)(2,1)}, u32[]{:S(2)}, u32[]{:S(2)}) %collective-permute-start.8) | collective-permute-done | bytes 1572896 | tf_op jit(solution)/shard_map/ppermute | solution.py:31
  60.9 2.3 %collective-permute-start.9 = (bf16[4,384,512]{2,1,0:T(8,128)(2,1)}, bf16[4,384,512]{2,1,0:T(8,128)(2,1)}, u32[]{:S(2)}, u32[]{:S(2)}) collective-permute-start(bf16[4,384,512]{2,1,0:T(8,128)(2,1)} %collective-permute-done.8.refs_1_), channel_id=1, source_target_pairs={{0,4},{1,5},{2,6},{3,7},{4,8},{5,9},{6,10},{7,11},{8,12},{9,13},{1... | collective-permute-start | bytes 4718600 | tf_op jit(solution)/shard_map/ppermute | solution.py:31
  63.2 4.1 %collective-permute-done.3.refs_0_ = bf16[4,384,512]{2,1,0:T(8,128)(2,1)} collective-permute-done((bf16[4,384,512]{2,1,0:T(8,128)(2,1)}, bf16[4,384,512]{2,1,0:T(8,128)(2,1)}, u32[]{:S(2)}, u32[]{:S(2)}) %collective-permute-start.3) | collective-permute-done | bytes 1572896 | tf_op jit(solution)/shard_map/ppermute | solution.py:31
  67.3 6.7 %all-to-all-done.parts_ref = f32[16,4,768]{2,1,0:T(4,128)S(1)} async-done(((f32[16,4,768]{2,1,0:T(4,128)}), f32[16,4,768]{2,1,0:T(4,128)S(1)}, u32[]{:S(2)}, u32[]{:S(2)}) %all-to-all-start) | async-done | bytes 196640 | tf_op jit(solution)/shard_map/all_to_all | solution.py:319
  74.1 0.8 collective-permute-start.4
  74.9 0.1 broadcast_in_dim_reshape.12.slot_ref
  75.0 0.1 broadcast_in_dim.34
  75.1 0.2 broadcast_in_dim_reshape.11.rank_ref
  75.3 0.7 reduce_ranks.1
  76.0 8.3 %all-to-all-start.1 = ((bf16[16,4,768]{2,1,0:T(4,128)(2,1)}), bf16[16,4,768]{2,1,0:T(4,128)(2,1)S(1)}, u32[]{:S(2)}, u32[]{:S(2)}) async-start(bf16[16,4,768]{2,1,0:T(4,128)(2,1)} %reduce_ranks.1), calls=%async_computation.1 | async-start | bytes 196608 | tf_op jit(solution)/shard_map/all_to_all | solution.py:323
  84.3 3.9 %base_dots.5.refs_3_ = f32[768,512]{1,0:T(8,128)S(1)} custom-call(bf16[4,384,512]{2,1,0:T(8,128)(2,1)} %collective-permute-done.3.refs_0_, bf16[4,384,512]{2,1,0:T(8,128)(2,1)} %collective-permute-done.8.refs_1_, bf16[8192,512]{1,0:T(8,128)(2,1)} %refs_2_.7, f32[768,512]{1,0:T(8,128)S(1)} %base_dots.4.refs_3_), custom_call_target="tpu_custom_call" | custom-call | flops 1610612736 | bytes 1048576 | tf_op jit(solution)/shard_map/base_dots/pallas_call | solution.py:161
  88.3 3.8 %base_dots.6.total_ref = f32[768,512]{1,0:T(8,128)S(1)} custom-call(bf16[4,384,512]{2,1,0:T(8,128)(2,1)} %collective-permute-done.10.refs_0_, bf16[4,384,512]{2,1,0:T(8,128)(2,1)} %collective-permute-done.11.refs_1_, bf16[8192,512]{1,0:T(8,128)(2,1)} %refs_2_.7, f32[768,512]{1,0:T(8,128)S(1)} %base_dots.5.refs_3_), custom_call_target="tpu_custom_call" | custom-call | flops 1610612736 | bytes 1048576 | tf_op jit(solution)/shard_map/base_dots/pallas_call | solution.py:161
  92.1 0.0 all-gather.5.cloned.1.call-done
  92.1 6.7 %all-to-all-done.1.reduced_ref = bf16[16,4,768]{2,1,0:T(4,128)(2,1)S(1)} async-done(((bf16[16,4,768]{2,1,0:T(4,128)(2,1)}), bf16[16,4,768]{2,1,0:T(4,128)(2,1)S(1)}, u32[]{:S(2)}, u32[]{:S(2)}) %all-to-all-start.1) | async-done | bytes 98336 | tf_op jit(solution)/shard_map/all_to_all | solution.py:323
  98.8 2.2 %copy-done.2 = bf16[64,64,512]{2,1,0:T(8,128)(2,1)S(1)} copy-done((bf16[64,64,512]{2,1,0:T(8,128)(2,1)S(1)}, bf16[64,64,512]{2,1,0:T(8,128)(2,1)}, u32[]{:S(2)}) %copy-start.2) | copy-done | bytes 4194328
  101.0 3.5 %add_lora.1.refs_3_ = f32[768,512]{1,0:T(8,128)S(1)} custom-call(s32[768,1]{1,0:T(8,128)S(1)} %broadcast_in_dim_reshape.12.slot_ref, bf16[16,4,768]{2,1,0:T(4,128)(2,1)S(1)} %all-to-all-done.1.reduced_ref, bf16[4096,512]{1,0:T(8,128)(2,1)S(1)} %bitcast.2, f32[768,512]{1,0:T(8,128)S(1)} %base_dots.6.total_ref), custom_call_target="tpu_custom_call" | custom-call | flops 3221225472 | bytes 1048576 | tf_op jit(solution)/shard_map/add_lora/pallas_call | solution.py:63
  104.5 4.7 %base_dots.7 = bf16[384,2,512]{2,1,0:T(2,128)(2,1)} custom-call(bf16[4,384,512]{2,1,0:T(8,128)(2,1)} %collective-permute-done.4.refs_0_, bf16[4,384,512]{2,1,0:T(8,128)(2,1)} %collective-permute-done.9.refs_1_, bf16[8192,512]{1,0:T(8,128)(2,1)} %refs_2_.7, f32[768,512]{1,0:T(8,128)S(1)} %add_lora.1.refs_3_), custom_call_target="tpu_custom_call" | custom-call | flops 1610612736 | bytes 1048576 | tf_op jit(solution)/shard_map/base_dots/pallas_call | solution.py:161
  (16 shorter events, 0.0 us)
Async XLA Ops:
  6.5 1.5 %copy-start.1 = (bf16[384,2,512]{2,1,0:T(2,128)(2,1)S(1)}, bf16[384,2,512]{2,1,0:T(2,128)(2,1)}, u32[]{:S(2)}) copy-start(bf16[384,2,512]{2,1,0:T(2,128)(2,1)} %hidden_ref.1) | copy-start | bytes 2359300
  6.5 34.1 %all-gather.3.cloned.1.call-start = ((), (), s32[]{:S(2)}) async-start(), calls=%async_computation.2 | async-start | bytes 4718592 | tf_op jit(solution)/shard_map/all_gather | solution.py:291
  7.3 84.8 %all-gather.5.cloned.1.call-start = ((), (), s32[]{:S(2)}) async-start(), calls=%async_computation.3 | async-start | bytes 4718592 | tf_op jit(solution)/shard_map/all_gather | solution.py:292
  8.2 0.9 copy-start.3
  9.1 9.0 %collective-permute-start.5 = (bf16[384,512]{1,0:T(8,128)(2,1)S(1)}, bf16[384,512]{1,0:T(8,128)(2,1)S(1)}, u32[]{:S(2)}, u32[]{:S(2)}) collective-permute-start(bf16[384,512]{1,0:T(8,128)(2,1)S(1)} %get-tuple-element.23.refs_0_), channel_id=1, source_target_pairs={{0,1},{1,2},{2,3},{3,0},{4,5},{5,6},{6,7},{7,4},{8,9},{9,10},{10,1... | collective-permute-start | bytes 1179656 | tf_op jit(solution)/shard_map/ppermute | solution.py:31
  10.6 11.5 %collective-permute-start = (bf16[384,512]{1,0:T(8,128)(2,1)S(1)}, bf16[384,512]{1,0:T(8,128)(2,1)S(1)}, u32[]{:S(2)}, u32[]{:S(2)}) collective-permute-start(bf16[384,512]{1,0:T(8,128)(2,1)S(1)} %get-tuple-element.18.refs_0_), channel_id=1, source_target_pairs={{0,4},{1,5},{2,6},{3,7},{4,8},{5,9},{6,10},{7,11},{8,12},{9,13},{1... | collective-permute-start | bytes 1179656 | tf_op jit(solution)/shard_map/ppermute | solution.py:31
  11.1 11.0 %collective-permute-start.6 = (bf16[384,512]{1,0:T(8,128)(2,1)S(1)}, bf16[384,512]{1,0:T(8,128)(2,1)S(1)}, u32[]{:S(2)}, u32[]{:S(2)}) collective-permute-start(bf16[384,512]{1,0:T(8,128)(2,1)S(1)} %get-tuple-element.23.refs_0_), channel_id=1, source_target_pairs={{0,3},{1,0},{2,1},{3,2},{4,7},{5,4},{6,5},{7,6},{8,11},{9,8},{10,9... | collective-permute-start | bytes 1179656 | tf_op jit(solution)/shard_map/ppermute | solution.py:31
  18.0 11.3 %collective-permute-start.7 = (bf16[384,512]{1,0:T(8,128)(2,1)S(1)}, bf16[384,512]{1,0:T(8,128)(2,1)S(1)}, u32[]{:S(2)}, u32[]{:S(2)}) collective-permute-start(bf16[384,512]{1,0:T(8,128)(2,1)S(1)} %collective-permute-done.5.refs_1_), channel_id=1, source_target_pairs={{0,1},{1,2},{2,3},{3,0},{4,5},{5,6},{6,7},{7,4},{8,9},{9,10},{10,1... | collective-permute-start | bytes 1179656 | tf_op jit(solution)/shard_map/ppermute | solution.py:31
  18.4 13.0 %collective-permute-start.1 = (bf16[384,512]{1,0:T(8,128)(2,1)S(1)}, bf16[384,512]{1,0:T(8,128)(2,1)S(1)}, u32[]{:S(2)}, u32[]{:S(2)}) collective-permute-start(bf16[384,512]{1,0:T(8,128)(2,1)S(1)} %get-tuple-element.18.refs_0_), channel_id=1, source_target_pairs={{0,12},{1,13},{2,14},{3,15},{4,0},{5,1},{6,2},{7,3},{8,4},{9,5},{1... | collective-permute-start | bytes 1179656 | tf_op jit(solution)/shard_map/ppermute | solution.py:31
  22.1 9.4 %collective-permute-start.2 = (bf16[384,512]{1,0:T(8,128)(2,1)S(1)}, bf16[384,512]{1,0:T(8,128)(2,1)S(1)}, u32[]{:S(2)}, u32[]{:S(2)}) collective-permute-start(bf16[384,512]{1,0:T(8,128)(2,1)S(1)} %collective-permute-done.refs_1_), channel_id=1, source_target_pairs={{0,4},{1,5},{2,6},{3,7},{4,8},{5,9},{6,10},{7,11},{8,12},{9,13},{1... | collective-permute-start | bytes 1179656 | tf_op jit(solution)/shard_map/ppermute | solution.py:31
  29.4 3.7 %copy-start = (bf16[4,384,512]{2,1,0:T(8,128)(2,1)}, bf16[4,384,512]{2,1,0:T(8,128)(2,1)S(1)}, u32[]{:S(2)}) copy-start(bf16[4,384,512]{2,1,0:T(8,128)(2,1)S(1)} %join.3.refs_1_) | copy-start | bytes 4718596
  29.4 3.3 %copy-start.4 = (s32[384]{0:T(512)S(1)}, s32[384]{0:T(512)}, u32[]{:S(2)}) copy-start(s32[384]{0:T(512)} %param.13) | copy-start | bytes 4612
  29.5 3.3 %copy-start.5 = (s32[64]{0:T(128)S(1)}, s32[64]{0:T(128)}, u32[]{:S(2)}) copy-start(s32[64]{0:T(128)} %param.11) | copy-start | bytes 772
  29.5 3.3 %copy-start.6 = (s32[64]{0:T(128)S(1)}, s32[64]{0:T(128)}, u32[]{:S(2)}) copy-start(s32[64]{0:T(128)} %param.12) | copy-start | bytes 772
  29.5 31.5 %collective-permute-start.8 = (bf16[4,384,512]{2,1,0:T(8,128)(2,1)S(1)}, bf16[4,384,512]{2,1,0:T(8,128)(2,1)}, u32[]{:S(2)}, u32[]{:S(2)}) collective-permute-start(bf16[4,384,512]{2,1,0:T(8,128)(2,1)S(1)} %join.3.refs_1_), channel_id=1, source_target_pairs={{0,4},{1,5},{2,6},{3,7},{4,8},{5,9},{6,10},{7,11},{8,12},{9,13},{1... | collective-permute-start | bytes 4718600 | tf_op jit(solution)/shard_map/ppermute | solution.py:31
  32.7 34.6 %collective-permute-start.3 = (bf16[4,384,512]{2,1,0:T(8,128)(2,1)}, bf16[4,384,512]{2,1,0:T(8,128)(2,1)}, u32[]{:S(2)}, u32[]{:S(2)}) collective-permute-start(bf16[4,384,512]{2,1,0:T(8,128)(2,1)} %join.2.refs_0_), channel_id=1, source_target_pairs={{0,1},{1,2},{2,3},{3,0},{4,5},{5,6},{6,7},{7,4},{8,9},{9,10},{10,1... | collective-permute-start | bytes 4718600 | tf_op jit(solution)/shard_map/ppermute | solution.py:31
  37.3 51.0 %collective-permute-start.10 = (bf16[4,384,512]{2,1,0:T(8,128)(2,1)}, bf16[4,384,512]{2,1,0:T(8,128)(2,1)}, u32[]{:S(2)}, u32[]{:S(2)}) collective-permute-start(bf16[4,384,512]{2,1,0:T(8,128)(2,1)} %join.2.refs_0_), channel_id=1, source_target_pairs={{0,3},{1,0},{2,1},{3,2},{4,7},{5,4},{6,5},{7,6},{8,11},{9,8},{10,9... | collective-permute-start | bytes 4718600 | tf_op jit(solution)/shard_map/ppermute | solution.py:31
  40.5 47.7 %collective-permute-start.11 = (bf16[4,384,512]{2,1,0:T(8,128)(2,1)}, bf16[4,384,512]{2,1,0:T(8,128)(2,1)}, u32[]{:S(2)}, u32[]{:S(2)}) collective-permute-start(bf16[4,384,512]{2,1,0:T(8,128)(2,1)} %copy-done), channel_id=1, source_target_pairs={{0,12},{1,13},{2,14},{3,15},{4,0},{5,1},{6,2},{7,3},{8,4},{9,5},{1... | collective-permute-start | bytes 4718600 | tf_op jit(solution)/shard_map/ppermute | solution.py:31
  47.1 26.9 %all-to-all-start = ((f32[16,4,768]{2,1,0:T(4,128)}), f32[16,4,768]{2,1,0:T(4,128)S(1)}, u32[]{:S(2)}, u32[]{:S(2)}) async-start(f32[16,4,768]{2,1,0:T(4,128)} %rank_scores.1), calls=%async_computation | async-start | bytes 393216 | tf_op jit(solution)/shard_map/all_to_all | solution.py:319
  60.9 43.6 %collective-permute-start.9 = (bf16[4,384,512]{2,1,0:T(8,128)(2,1)}, bf16[4,384,512]{2,1,0:T(8,128)(2,1)}, u32[]{:S(2)}, u32[]{:S(2)}) collective-permute-start(bf16[4,384,512]{2,1,0:T(8,128)(2,1)} %collective-permute-done.8.refs_1_), channel_id=1, source_target_pairs={{0,4},{1,5},{2,6},{3,7},{4,8},{5,9},{6,10},{7,11},{8,12},{9,13},{1... | collective-permute-start | bytes 4718600 | tf_op jit(solution)/shard_map/ppermute | solution.py:31
  74.1 30.4 %collective-permute-start.4 = (bf16[4,384,512]{2,1,0:T(8,128)(2,1)}, bf16[4,384,512]{2,1,0:T(8,128)(2,1)}, u32[]{:S(2)}, u32[]{:S(2)}) collective-permute-start(bf16[4,384,512]{2,1,0:T(8,128)(2,1)} %collective-permute-done.3.refs_0_), channel_id=1, source_target_pairs={{0,1},{1,2},{2,3},{3,0},{4,5},{5,6},{6,7},{7,4},{8,9},{9,10},{10,1... | collective-permute-start | bytes 4718600 | tf_op jit(solution)/shard_map/ppermute | solution.py:31
  76.0 22.8 %all-to-all-start.1 = ((bf16[16,4,768]{2,1,0:T(4,128)(2,1)}), bf16[16,4,768]{2,1,0:T(4,128)(2,1)S(1)}, u32[]{:S(2)}, u32[]{:S(2)}) async-start(bf16[16,4,768]{2,1,0:T(4,128)(2,1)} %reduce_ranks.1), calls=%async_computation.1 | async-start | bytes 196608 | tf_op jit(solution)/shard_map/all_to_all | solution.py:323
  98.8 2.2 %copy-start.2 = (bf16[64,64,512]{2,1,0:T(8,128)(2,1)S(1)}, bf16[64,64,512]{2,1,0:T(8,128)(2,1)}, u32[]{:S(2)}) copy-start(bf16[64,64,512]{2,1,0:T(8,128)(2,1)} %all-gather.5.cloned.1.call-done) | copy-start | bytes 12582916
Sparse Core Ops, SparseCore 0:
  9.1 31.3 all-gather.2
  42.2 32.1 all-gather.4

commit v4 on v3

--- a/solution.py
+++ b/solution.py
@@ -313,7 +313,7 @@
     first_ahead = send(first_line, 0, 1)
     second_ahead = send(second_line, 1, 0)
     total = base_dots(both(first_line, second_line, 0), base_matrix, None)
-    first_back = send(first_line, 0, -1, waits=[total])
+    first_back = send(first_line, 0, -1)
     second_back = send(second_line, -1, 0)
     partial = rank_scores(slot[None, :], rows, down, tp_size)
     parts = lax.all_to_all(partial, "tp", 0, 0, tiled=True)

time: 116 us -> 116 us (level); the launches traced: 116 us -> 115 us
  starting transfers between devices: 28.8 us -> 26.9 us
  waiting for transfers between devices: 41.1 us -> 39.9 us
    all_to_all x1, waiting for transfers between devices: 6.72 us -> 1.84 us  [per_device(): reduced = lax.all_to_all(spread, 'tp', 0, 0, tiled=True)]
    all_to_all x1, waiting for transfers between devices: 6.74 us -> 2.75 us  [per_device(): parts = lax.all_to_all(partial, 'tp', 0, 0, tiled=True)]
    all_gather x1, waiting for transfers between devices: 0.01 us -> 3.87 us  [per_device(): down = lax.all_gather(adapter_down, 'group', axis=0, tiled=True)]
    ppermute x12, waiting for transfers between devices: 26.2 us -> 30 us  [shift(): return lax.ppermute(value, BOTH, shift_pairs(dx, dy))]
    all_to_all x1, starting transfers between devices: 8.33 us -> 6.89 us  [per_device(): reduced = lax.all_to_all(spread, 'tp', 0, 0, tiled=True)]
    unnamed x14 -> x16, local copies, waits for them, and re-layouts: 3.09 us -> 3.1 us
  transfers between devices with their start and end apart: 16 -> 16, of which waited for: 7 -> 8; matrix products, arithmetic and copies ran while one was open for 1% -> 1% of each run, Pallas kernels for 21% -> 22%
where the time goes in v4:
time: 116 us; the launch traced here: 115 us
  waiting for transfers between devices  39.9 us (34%)
  Pallas kernels  29.8 us (26%)
  starting transfers between devices  26.9 us (23%)
  between operations  13.6 us (12%)
  local copies, waits for them, and re-layouts  4.5 us (4%)
    ppermute x12, waiting for transfers between devices, shift(): return lax.ppermute(value, BOTH, shift_pairs(dx, dy))  30 us
    pallas_call x4, Pallas kernels, base_dots(): pl.pallas_call(functools.partial(base_body, names, total is not None), in...  16.7 us
    ppermute x12, starting transfers between devices, shift(): return lax.ppermute(value, BOTH, shift_pairs(dx, dy))  12.7 us
    all_to_all x1, starting transfers between devices, per_device(): parts = lax.all_to_all(partial, 'tp', 0, 0, tiled=True)  7.26 us
    all_to_all x1, starting transfers between devices, per_device(): reduced = lax.all_to_all(spread, 'tp', 0, 0, tiled=True)  6.89 us
    pallas_call x5, Pallas kernels, local_call(): pl.pallas_call(body, in_specs=[pl.BlockSpec(memory_space=pltpu.VMEM)] * l...  6.64 us
    pallas_call x1, Pallas kernels, rank_scores(): pl.pallas_call(functools.partial(scores_body, rank_width), grid=(pages //...  6.49 us
    all_gather x1, waiting for transfers between devices, per_device(): down = lax.all_gather(adapter_down, 'group', axis=0, tiled=True)  3.87 us
  transfers between devices with their start and end apart: 16, of which 8 were waited for; matrix products, arithmetic and copies ran while one was open for 1% of the time, Pallas kernels for 22%

profile of v4, /device:TPU:102, one launch (start us, length us, event | category | flops | bytes accessed | tf_op | source)
XLA Modules:
  0.0 114.8 jit_solution(5071541342965922932)
XLA Ops:
  6.5 0.7 all-gather.3.cloned.1.call-update
  7.3 0.0 all-gather.5.cloned.1.call-start
  7.3 0.7 all-gather.5.cloned.1.call-update
  8.0 0.2 flatten.1
  8.2 0.0 copy-start.4
  8.2 0.9 copy-done.4
  9.1 1.6 %collective-permute-start.5 = (bf16[384,512]{1,0:T(8,128)(2,1)S(1)}, bf16[384,512]{1,0:T(8,128)(2,1)S(1)}, u32[]{:S(2)}, u32[]{:S(2)}) collective-permute-start(bf16[384,512]{1,0:T(8,128)(2,1)S(1)} %get-tuple-element.23.refs_0_), channel_id=1, source_target_pairs={{0,1},{1,2},{2,3},{3,0},{4,5},{5,6},{6,7},{7,4},{8,9},{9,10},{10,1... | collective-permute-start | bytes 1179656 | tf_op jit(solution)/shard_map/ppermute | solution.py:31
  10.6 0.5 collective-permute-start
  11.1 1.7 %collective-permute-start.6 = (bf16[384,512]{1,0:T(8,128)(2,1)S(1)}, bf16[384,512]{1,0:T(8,128)(2,1)S(1)}, u32[]{:S(2)}, u32[]{:S(2)}) collective-permute-start(bf16[384,512]{1,0:T(8,128)(2,1)S(1)} %get-tuple-element.23.refs_0_), channel_id=1, source_target_pairs={{0,3},{1,0},{2,1},{3,2},{4,7},{5,4},{6,5},{7,6},{8,11},{9,8},{10,9... | collective-permute-start | bytes 1179656 | tf_op jit(solution)/shard_map/ppermute | solution.py:31
  12.8 5.3 %collective-permute-done.5.refs_1_ = bf16[384,512]{1,0:T(8,128)(2,1)S(1)} collective-permute-done((bf16[384,512]{1,0:T(8,128)(2,1)S(1)}, bf16[384,512]{1,0:T(8,128)(2,1)S(1)}, u32[]{:S(2)}, u32[]{:S(2)}) %collective-permute-start.5) | collective-permute-done | bytes 393248 | tf_op jit(solution)/shard_map/ppermute | solution.py:31
  18.0 0.4 collective-permute-start.7
  18.4 0.8 collective-permute-start.1
  19.2 2.9 %collective-permute-done.refs_1_ = bf16[384,512]{1,0:T(8,128)(2,1)S(1)} collective-permute-done((bf16[384,512]{1,0:T(8,128)(2,1)S(1)}, bf16[384,512]{1,0:T(8,128)(2,1)S(1)}, u32[]{:S(2)}, u32[]{:S(2)}) %collective-permute-start) | collective-permute-done | bytes 393248 | tf_op jit(solution)/shard_map/ppermute | solution.py:31
  22.1 0.0 collective-permute-start.2
  22.1 7.2 %collective-permute-done.7.refs_3_ = bf16[384,512]{1,0:T(8,128)(2,1)S(1)} collective-permute-done((bf16[384,512]{1,0:T(8,128)(2,1)S(1)}, bf16[384,512]{1,0:T(8,128)(2,1)S(1)}, u32[]{:S(2)}, u32[]{:S(2)}) %collective-permute-start.7) | collective-permute-done | bytes 393248 | tf_op jit(solution)/shard_map/ppermute | solution.py:31
  29.3 0.1 join.3.refs_1_
  29.4 0.0 copy-start.5
  29.5 0.0 copy-start.6
  29.5 0.0 copy-start.7
  29.5 2.0 %collective-permute-start.8 = (bf16[4,384,512]{2,1,0:T(8,128)(2,1)S(1)}, bf16[4,384,512]{2,1,0:T(8,128)(2,1)}, u32[]{:S(2)}, u32[]{:S(2)}) collective-permute-start(bf16[4,384,512]{2,1,0:T(8,128)(2,1)S(1)} %join.3.refs_1_), channel_id=1, source_target_pairs={{0,4},{1,5},{2,6},{3,7},{4,8},{5,9},{6,10},{7,11},{8,12},{9,13},{1... | collective-permute-start | bytes 4718600 | tf_op jit(solution)/shard_map/ppermute | solution.py:31
  31.5 1.3 %join.2.refs_0_ = bf16[4,384,512]{2,1,0:T(8,128)(2,1)} custom-call(bf16[384,512]{1,0:T(8,128)(2,1)S(1)} %get-tuple-element.18.refs_0_, bf16[384,512]{1,0:T(8,128)(2,1)S(1)} %collective-permute-done.refs_1_, bf16[384,512]{1,0:T(8,128)(2,1)S(1)} %collective-permute-done.1.refs_2_, bf16[384,512]{1,0:T(8,128)(2,1)S(1)} %collective-permute-done.2.refs_3_), custom_call_target="tpu_custom_call" | custom-call | bytes 1048576 | tf_op jit(solution)/shard_map/join/pallas_call | solution.py:63
  32.8 0.1 select_reduce_fusion
  32.9 0.1 broadcast_in_dim.32
  33.0 0.2 broadcast_in_dim_reshape.9.slot_ref
  33.2 0.2 collective-permute-start.11
  33.4 3.2 %collective-permute-start.10 = (bf16[4,384,512]{2,1,0:T(8,128)(2,1)}, bf16[4,384,512]{2,1,0:T(8,128)(2,1)}, u32[]{:S(2)}, u32[]{:S(2)}) collective-permute-start(bf16[4,384,512]{2,1,0:T(8,128)(2,1)} %join.2.refs_0_), channel_id=1, source_target_pairs={{0,3},{1,0},{2,1},{3,2},{4,7},{5,4},{6,5},{7,6},{8,11},{9,8},{10,9... | collective-permute-start | bytes 4718600 | tf_op jit(solution)/shard_map/ppermute | solution.py:31
  36.6 3.9 %all-gather.3.cloned.1.call-done = bf16[64,64,512]{2,1,0:T(8,128)(2,1)} async-done(((bf16[8,64,512]{2,1,0:T(8,128)(2,1)}), bf16[64,64,512]{2,1,0:T(8,128)(2,1)}) %all-gather.3.cloned.1.call-update) | async-done | bytes 4194320 | tf_op jit(solution)/shard_map/all_gather | solution.py:291
  40.5 6.5 %rank_scores.1 = f32[16,4,768]{2,1,0:T(4,128)} custom-call(s32[1,768]{1,0:T(1,128)S(1)} %broadcast_in_dim_reshape.9.slot_ref, bf16[768,512]{1,0:T(8,128)(2,1)} %copy-done.4, bf16[4096,512]{1,0:T(8,128)(2,1)} %bitcast.3), custom_call_target="tpu_custom_call" | custom-call | flops 3221225472 | bytes 5242880 | tf_op jit(solution)/shard_map/rank_scores/pallas_call | solution.py:213
  47.0 7.3 %all-to-all-start = ((f32[16,4,768]{2,1,0:T(4,128)}), f32[16,4,768]{2,1,0:T(4,128)S(1)}, u32[]{:S(2)}, u32[]{:S(2)}) async-start(f32[16,4,768]{2,1,0:T(4,128)} %rank_scores.1), calls=%async_computation | async-start | bytes 393216 | tf_op jit(solution)/shard_map/all_to_all | solution.py:319
  54.2 10.9 %collective-permute-done.8.refs_1_ = bf16[4,384,512]{2,1,0:T(8,128)(2,1)} collective-permute-done((bf16[4,384,512]{2,1,0:T(8,128)(2,1)S(1)}, bf16[4,384,512]{2,1,0:T(8,128)(2,1)}, u32[]{:S(2)}, u32[]{:S(2)}) %collective-permute-start.8) | collective-permute-done | bytes 1572896 | tf_op jit(solution)/shard_map/ppermute | solution.py:31
  65.1 2.1 %collective-permute-start.9 = (bf16[4,384,512]{2,1,0:T(8,128)(2,1)}, bf16[4,384,512]{2,1,0:T(8,128)(2,1)}, u32[]{:S(2)}, u32[]{:S(2)}) collective-permute-start(bf16[4,384,512]{2,1,0:T(8,128)(2,1)} %collective-permute-done.8.refs_1_), channel_id=1, source_target_pairs={{0,4},{1,5},{2,6},{3,7},{4,8},{5,9},{6,10},{7,11},{8,12},{9,13},{1... | collective-permute-start | bytes 4718600 | tf_op jit(solution)/shard_map/ppermute | solution.py:31
  67.2 3.8 %collective-permute-done.3.refs_0_ = bf16[4,384,512]{2,1,0:T(8,128)(2,1)} collective-permute-done((bf16[4,384,512]{2,1,0:T(8,128)(2,1)}, bf16[4,384,512]{2,1,0:T(8,128)(2,1)}, u32[]{:S(2)}, u32[]{:S(2)}) %collective-permute-start.3) | collective-permute-done | bytes 1572896 | tf_op jit(solution)/shard_map/ppermute | solution.py:31
  70.9 2.8 %all-to-all-done.parts_ref = f32[16,4,768]{2,1,0:T(4,128)S(1)} async-done(((f32[16,4,768]{2,1,0:T(4,128)}), f32[16,4,768]{2,1,0:T(4,128)S(1)}, u32[]{:S(2)}, u32[]{:S(2)}) %all-to-all-start) | async-done | bytes 196640 | tf_op jit(solution)/shard_map/all_to_all | solution.py:319
  73.7 0.3 collective-permute-start.4
  74.0 0.9 broadcast_in_dim_reshape.12.slot_ref
  74.9 0.1 broadcast_in_dim.34
  75.0 0.2 broadcast_in_dim_reshape.11.rank_ref
  75.2 4.2 %base_dots.4.refs_3_ = f32[768,512]{1,0:T(8,128)S(1)} custom-call(bf16[4,384,512]{2,1,0:T(8,128)(2,1)} %join.2.refs_0_, bf16[4,384,512]{2,1,0:T(8,128)(2,1)} %copy-done, bf16[8192,512]{1,0:T(8,128)(2,1)} %refs_2_.7), custom_call_target="tpu_custom_call" | custom-call | flops 1610612736 | bytes 1048576 | tf_op jit(solution)/shard_map/base_dots/pallas_call | solution.py:161
  79.4 0.7 reduce_ranks.1
  80.1 6.9 %all-to-all-start.1 = ((bf16[16,4,768]{2,1,0:T(4,128)(2,1)}), bf16[16,4,768]{2,1,0:T(4,128)(2,1)}, u32[]{:S(2)}, u32[]{:S(2)}) async-start(bf16[16,4,768]{2,1,0:T(4,128)(2,1)} %reduce_ranks.1), calls=%async_computation.1 | async-start | bytes 196608 | tf_op jit(solution)/shard_map/all_to_all | solution.py:323
  87.0 3.9 %base_dots.5.refs_3_ = f32[768,512]{1,0:T(8,128)S(1)} custom-call(bf16[4,384,512]{2,1,0:T(8,128)(2,1)} %collective-permute-done.3.refs_0_, bf16[4,384,512]{2,1,0:T(8,128)(2,1)} %collective-permute-done.8.refs_1_, bf16[8192,512]{1,0:T(8,128)(2,1)} %refs_2_.7, f32[768,512]{1,0:T(8,128)S(1)} %base_dots.4.refs_3_), custom_call_target="tpu_custom_call" | custom-call | flops 1610612736 | bytes 1048576 | tf_op jit(solution)/shard_map/base_dots/pallas_call | solution.py:161
  90.9 0.0 copy-start.2
  91.0 3.9 %base_dots.6.total_ref = f32[768,512]{1,0:T(8,128)S(1)} custom-call(bf16[4,384,512]{2,1,0:T(8,128)(2,1)} %collective-permute-done.10.refs_0_, bf16[4,384,512]{2,1,0:T(8,128)(2,1)} %collective-permute-done.11.refs_1_, bf16[8192,512]{1,0:T(8,128)(2,1)} %refs_2_.7, f32[768,512]{1,0:T(8,128)S(1)} %base_dots.5.refs_3_), custom_call_target="tpu_custom_call" | custom-call | flops 1610612736 | bytes 1048576 | tf_op jit(solution)/shard_map/base_dots/pallas_call | solution.py:161
  94.8 0.0 all-gather.5.cloned.1.call-done
  94.9 1.8 %all-to-all-done.1.reduced_ref = bf16[16,4,768]{2,1,0:T(4,128)(2,1)} async-done(((bf16[16,4,768]{2,1,0:T(4,128)(2,1)}), bf16[16,4,768]{2,1,0:T(4,128)(2,1)}, u32[]{:S(2)}, u32[]{:S(2)}) %all-to-all-start.1) | async-done | bytes 98336 | tf_op jit(solution)/shard_map/all_to_all | solution.py:323
  96.7 2.2 %copy-done.3 = bf16[64,64,512]{2,1,0:T(8,128)(2,1)S(1)} copy-done((bf16[64,64,512]{2,1,0:T(8,128)(2,1)S(1)}, bf16[64,64,512]{2,1,0:T(8,128)(2,1)}, u32[]{:S(2)}) %copy-start.3) | copy-done | bytes 4194328
  98.9 4.4 %add_lora.1.refs_3_ = f32[768,512]{1,0:T(8,128)S(1)} custom-call(s32[768,1]{1,0:T(8,128)S(1)} %copy-done.2, bf16[16,4,768]{2,1,0:T(4,128)(2,1)} %all-to-all-done.1.reduced_ref, bf16[4096,512]{1,0:T(8,128)(2,1)S(1)} %bitcast.2, f32[768,512]{1,0:T(8,128)S(1)} %base_dots.6.total_ref), custom_call_target="tpu_custom_call" | custom-call | flops 3221225472 | bytes 1048576 | tf_op jit(solution)/shard_map/add_lora/pallas_call | solution.py:63
  103.3 4.7 %base_dots.7 = bf16[384,2,512]{2,1,0:T(2,128)(2,1)} custom-call(bf16[4,384,512]{2,1,0:T(8,128)(2,1)} %collective-permute-done.4.refs_0_, bf16[4,384,512]{2,1,0:T(8,128)(2,1)} %collective-permute-done.9.refs_1_, bf16[8192,512]{1,0:T(8,128)(2,1)} %refs_2_.7, f32[768,512]{1,0:T(8,128)S(1)} %add_lora.1.refs_3_), custom_call_target="tpu_custom_call" | custom-call | flops 1610612736 | bytes 1048576 | tf_op jit(solution)/shard_map/base_dots/pallas_call | solution.py:161
  (18 shorter events, 0.0 us)
Async XLA Ops:
  6.5 1.5 %copy-start.1 = (bf16[384,2,512]{2,1,0:T(2,128)(2,1)S(1)}, bf16[384,2,512]{2,1,0:T(2,128)(2,1)}, u32[]{:S(2)}) copy-start(bf16[384,2,512]{2,1,0:T(2,128)(2,1)} %hidden_ref.1) | copy-start | bytes 2359300
  6.5 33.9 %all-gather.3.cloned.1.call-start = ((), (), s32[]{:S(2)}) async-start(), calls=%async_computation.2 | async-start | bytes 4718592 | tf_op jit(solution)/shard_map/all_gather | solution.py:291
  7.3 87.6 %all-gather.5.cloned.1.call-start = ((), (), s32[]{:S(2)}) async-start(), calls=%async_computation.3 | async-start | bytes 4718592 | tf_op jit(solution)/shard_map/all_gather | solution.py:292
  8.2 0.9 copy-start.4
  9.1 9.0 %collective-permute-start.5 = (bf16[384,512]{1,0:T(8,128)(2,1)S(1)}, bf16[384,512]{1,0:T(8,128)(2,1)S(1)}, u32[]{:S(2)}, u32[]{:S(2)}) collective-permute-start(bf16[384,512]{1,0:T(8,128)(2,1)S(1)} %get-tuple-element.23.refs_0_), channel_id=1, source_target_pairs={{0,1},{1,2},{2,3},{3,0},{4,5},{5,6},{6,7},{7,4},{8,9},{9,10},{10,1... | collective-permute-start | bytes 1179656 | tf_op jit(solution)/shard_map/ppermute | solution.py:31
  10.6 11.5 %collective-permute-start = (bf16[384,512]{1,0:T(8,128)(2,1)S(1)}, bf16[384,512]{1,0:T(8,128)(2,1)S(1)}, u32[]{:S(2)}, u32[]{:S(2)}) collective-permute-start(bf16[384,512]{1,0:T(8,128)(2,1)S(1)} %get-tuple-element.18.refs_0_), channel_id=1, source_target_pairs={{0,4},{1,5},{2,6},{3,7},{4,8},{5,9},{6,10},{7,11},{8,12},{9,13},{1... | collective-permute-start | bytes 1179656 | tf_op jit(solution)/shard_map/ppermute | solution.py:31
  11.1 11.0 %collective-permute-start.6 = (bf16[384,512]{1,0:T(8,128)(2,1)S(1)}, bf16[384,512]{1,0:T(8,128)(2,1)S(1)}, u32[]{:S(2)}, u32[]{:S(2)}) collective-permute-start(bf16[384,512]{1,0:T(8,128)(2,1)S(1)} %get-tuple-element.23.refs_0_), channel_id=1, source_target_pairs={{0,3},{1,0},{2,1},{3,2},{4,7},{5,4},{6,5},{7,6},{8,11},{9,8},{10,9... | collective-permute-start | bytes 1179656 | tf_op jit(solution)/shard_map/ppermute | solution.py:31
  18.0 11.3 %collective-permute-start.7 = (bf16[384,512]{1,0:T(8,128)(2,1)S(1)}, bf16[384,512]{1,0:T(8,128)(2,1)S(1)}, u32[]{:S(2)}, u32[]{:S(2)}) collective-permute-start(bf16[384,512]{1,0:T(8,128)(2,1)S(1)} %collective-permute-done.5.refs_1_), channel_id=1, source_target_pairs={{0,1},{1,2},{2,3},{3,0},{4,5},{5,6},{6,7},{7,4},{8,9},{9,10},{10,1... | collective-permute-start | bytes 1179656 | tf_op jit(solution)/shard_map/ppermute | solution.py:31
  18.4 13.0 %collective-permute-start.1 = (bf16[384,512]{1,0:T(8,128)(2,1)S(1)}, bf16[384,512]{1,0:T(8,128)(2,1)S(1)}, u32[]{:S(2)}, u32[]{:S(2)}) collective-permute-start(bf16[384,512]{1,0:T(8,128)(2,1)S(1)} %get-tuple-element.18.refs_0_), channel_id=1, source_target_pairs={{0,12},{1,13},{2,14},{3,15},{4,0},{5,1},{6,2},{7,3},{8,4},{9,5},{1... | collective-permute-start | bytes 1179656 | tf_op jit(solution)/shard_map/ppermute | solution.py:31
  22.1 9.4 %collective-permute-start.2 = (bf16[384,512]{1,0:T(8,128)(2,1)S(1)}, bf16[384,512]{1,0:T(8,128)(2,1)S(1)}, u32[]{:S(2)}, u32[]{:S(2)}) collective-permute-start(bf16[384,512]{1,0:T(8,128)(2,1)S(1)} %collective-permute-done.refs_1_), channel_id=1, source_target_pairs={{0,4},{1,5},{2,6},{3,7},{4,8},{5,9},{6,10},{7,11},{8,12},{9,13},{1... | collective-permute-start | bytes 1179656 | tf_op jit(solution)/shard_map/ppermute | solution.py:31
  29.4 3.8 %copy-start = (bf16[4,384,512]{2,1,0:T(8,128)(2,1)}, bf16[4,384,512]{2,1,0:T(8,128)(2,1)S(1)}, u32[]{:S(2)}) copy-start(bf16[4,384,512]{2,1,0:T(8,128)(2,1)S(1)} %join.3.refs_1_) | copy-start | bytes 4718596
  29.4 3.4 %copy-start.5 = (s32[384]{0:T(512)S(1)}, s32[384]{0:T(512)}, u32[]{:S(2)}) copy-start(s32[384]{0:T(512)} %param.13) | copy-start | bytes 4612
  29.5 3.4 %copy-start.6 = (s32[64]{0:T(128)S(1)}, s32[64]{0:T(128)}, u32[]{:S(2)}) copy-start(s32[64]{0:T(128)} %param.11) | copy-start | bytes 772
  29.5 3.4 %copy-start.7 = (s32[64]{0:T(128)S(1)}, s32[64]{0:T(128)}, u32[]{:S(2)}) copy-start(s32[64]{0:T(128)} %param.12) | copy-start | bytes 772
  29.5 35.6 %collective-permute-start.8 = (bf16[4,384,512]{2,1,0:T(8,128)(2,1)S(1)}, bf16[4,384,512]{2,1,0:T(8,128)(2,1)}, u32[]{:S(2)}, u32[]{:S(2)}) collective-permute-start(bf16[4,384,512]{2,1,0:T(8,128)(2,1)S(1)} %join.3.refs_1_), channel_id=1, source_target_pairs={{0,4},{1,5},{2,6},{3,7},{4,8},{5,9},{6,10},{7,11},{8,12},{9,13},{1... | collective-permute-start | bytes 4718600 | tf_op jit(solution)/shard_map/ppermute | solution.py:31
  32.8 38.1 %collective-permute-start.3 = (bf16[4,384,512]{2,1,0:T(8,128)(2,1)}, bf16[4,384,512]{2,1,0:T(8,128)(2,1)}, u32[]{:S(2)}, u32[]{:S(2)}) collective-permute-start(bf16[4,384,512]{2,1,0:T(8,128)(2,1)} %join.2.refs_0_), channel_id=1, source_target_pairs={{0,1},{1,2},{2,3},{3,0},{4,5},{5,6},{6,7},{7,4},{8,9},{9,10},{10,1... | collective-permute-start | bytes 4718600 | tf_op jit(solution)/shard_map/ppermute | solution.py:31
  33.2 57.7 %collective-permute-start.11 = (bf16[4,384,512]{2,1,0:T(8,128)(2,1)S(1)}, bf16[4,384,512]{2,1,0:T(8,128)(2,1)}, u32[]{:S(2)}, u32[]{:S(2)}) collective-permute-start(bf16[4,384,512]{2,1,0:T(8,128)(2,1)S(1)} %join.3.refs_1_), channel_id=1, source_target_pairs={{0,12},{1,13},{2,14},{3,15},{4,0},{5,1},{6,2},{7,3},{8,4},{9,5},{1... | collective-permute-start | bytes 4718600 | tf_op jit(solution)/shard_map/ppermute | solution.py:31
  33.4 57.6 %collective-permute-start.10 = (bf16[4,384,512]{2,1,0:T(8,128)(2,1)}, bf16[4,384,512]{2,1,0:T(8,128)(2,1)}, u32[]{:S(2)}, u32[]{:S(2)}) collective-permute-start(bf16[4,384,512]{2,1,0:T(8,128)(2,1)} %join.2.refs_0_), channel_id=1, source_target_pairs={{0,3},{1,0},{2,1},{3,2},{4,7},{5,4},{6,5},{7,6},{8,11},{9,8},{10,9... | collective-permute-start | bytes 4718600 | tf_op jit(solution)/shard_map/ppermute | solution.py:31
  47.0 26.7 %all-to-all-start = ((f32[16,4,768]{2,1,0:T(4,128)}), f32[16,4,768]{2,1,0:T(4,128)S(1)}, u32[]{:S(2)}, u32[]{:S(2)}) async-start(f32[16,4,768]{2,1,0:T(4,128)} %rank_scores.1), calls=%async_computation | async-start | bytes 393216 | tf_op jit(solution)/shard_map/all_to_all | solution.py:319
  65.1 38.2 %collective-permute-start.9 = (bf16[4,384,512]{2,1,0:T(8,128)(2,1)}, bf16[4,384,512]{2,1,0:T(8,128)(2,1)}, u32[]{:S(2)}, u32[]{:S(2)}) collective-permute-start(bf16[4,384,512]{2,1,0:T(8,128)(2,1)} %collective-permute-done.8.refs_1_), channel_id=1, source_target_pairs={{0,4},{1,5},{2,6},{3,7},{4,8},{5,9},{6,10},{7,11},{8,12},{9,13},{1... | collective-permute-start | bytes 4718600 | tf_op jit(solution)/shard_map/ppermute | solution.py:31
  73.7 29.6 %collective-permute-start.4 = (bf16[4,384,512]{2,1,0:T(8,128)(2,1)}, bf16[4,384,512]{2,1,0:T(8,128)(2,1)}, u32[]{:S(2)}, u32[]{:S(2)}) collective-permute-start(bf16[4,384,512]{2,1,0:T(8,128)(2,1)} %collective-permute-done.3.refs_0_), channel_id=1, source_target_pairs={{0,1},{1,2},{2,3},{3,0},{4,5},{5,6},{6,7},{7,4},{8,9},{9,10},{10,1... | collective-permute-start | bytes 4718600 | tf_op jit(solution)/shard_map/ppermute | solution.py:31
  80.1 16.6 %all-to-all-start.1 = ((bf16[16,4,768]{2,1,0:T(4,128)(2,1)}), bf16[16,4,768]{2,1,0:T(4,128)(2,1)}, u32[]{:S(2)}, u32[]{:S(2)}) async-start(bf16[16,4,768]{2,1,0:T(4,128)(2,1)} %reduce_ranks.1), calls=%async_computation.1 | async-start | bytes 196608 | tf_op jit(solution)/shard_map/all_to_all | solution.py:323
  90.9 5.8 %copy-start.2 = (s32[768,1]{1,0:T(8,128)S(1)}, s32[768,1]{1,0:T(8,128)}, u32[]{:S(2)}) copy-start(s32[768,1]{1,0:T(8,128)} %broadcast_in_dim_reshape.12.slot_ref) | copy-start | bytes 9220
  96.7 2.2 %copy-start.3 = (bf16[64,64,512]{2,1,0:T(8,128)(2,1)S(1)}, bf16[64,64,512]{2,1,0:T(8,128)(2,1)}, u32[]{:S(2)}) copy-start(bf16[64,64,512]{2,1,0:T(8,128)(2,1)} %all-gather.5.cloned.1.call-done) | copy-start | bytes 12582916
Sparse Core Ops, SparseCore 0:
  9.1 31.3 all-gather.2
  42.2 32.1 all-gather.4
